TPU v7x, 512 devices: a whole 4x4x16 slice. The times are simulated.
512 devices in a mesh: ctx: 64 (over z, y_lo, core), head: 8 (over x, y_hi).
Axes of the slice: x: 4, y: 4 (y_hi: 2, y_lo: 2; y = y_hi * 2 + y_lo), z: 16, core: 2. Of those that a mesh axis runs over, the one named last changes fastest.
Arguments:
- embeddings: bfloat16 [16384, 8192], P('ctx', 'head'), may hold values from -6 to 6
- adapter_down: bfloat16 [8192, 8], P('head'), may hold values from -0.0625 to 0.0625
- adapter_up: bfloat16 [8, 8192], P(None, 'head'), may hold values from -0.8984375 to 0.8984375
- query_base: bfloat16 [16384, 8192], P('ctx', 'head'), may hold values from -24 to 24
- key_states: bfloat16 [16384, 1024], P('ctx', 'head'), may hold values from -24 to 24
- values: bfloat16 [16384, 1024], P('ctx', 'head'), may hold values from -6 to 6
- grad_out: bfloat16 [16384, 8192], P('ctx', 'head'), may hold values from -36 to 36
Outputs:
- attn_out: bfloat16 [16384, 8192], P('ctx', 'head')
- grad_embeddings: float32 [16384, 8192], P('ctx', 'head')
- grad_adapter_down: float32 [8192, 8], P('head')
- grad_adapter_up: float32 [8, 8192], P(None, 'head')
- grad_key_states: float32 [16384, 1024], P('ctx', 'head')
- grad_values: float32 [16384, 1024], P('ctx', 'head')
All inputs are finite; a program needn't handle non-finite values.
Results may differ from a plain program's by a relative error of at most 0.0095.
The roundings to bfloat16 on the way count: a program that leaves them out, or rounds other values in their place, can miss the bound.
Values may be sent and summed in bfloat16 or wider, within the bound.
No kernel may reach another device: no remote copies, remote signals or barrier semaphores. Data moves between devices by JAX's collectives and lax.ppermute only.
A program may use at most 64 MiB of HBM per device.

v0:
```python
import math

import jax
import jax.numpy as jnp
from jax import lax
from jax.sharding import PartitionSpec as P

HD = 128
SPAN = 4


def from_behind(block, axis, distance):
    devices = range(lax.axis_size(axis))
    route = [((i - distance) % len(devices), i) for i in devices]
    return lax.ppermute(block, axis, route)


def block_pass(query_block, cot_block, mask_block, key_head, value_head):
    inv_scale = 1.0 / math.sqrt(HD)
    scores = (
        jnp.einsum("tqd,sd->tqs", query_block, key_head, preferred_element_type=jnp.float32)
        * inv_scale
    )
    scores = jnp.where(mask_block[:, None, :], scores, -1e30)
    top = jnp.max(scores, axis=-1, keepdims=True)
    weight = jnp.exp(scores - top)
    weight = weight / jnp.sum(weight, axis=-1, keepdims=True)
    weight_b = weight.astype(jnp.bfloat16)
    attn_full = jnp.einsum("tqs,sd->tqd", weight_b, value_head, preferred_element_type=jnp.float32)
    delta = jnp.sum(cot_block.astype(jnp.float32) * attn_full, axis=-1, keepdims=True)
    dprob = jnp.einsum("tqd,sd->tqs", cot_block, value_head, preferred_element_type=jnp.float32)
    dscore = (weight * (dprob - delta)).astype(jnp.bfloat16)
    grad_q = (
        jnp.einsum("tqs,sd->tqd", dscore, key_head, preferred_element_type=jnp.float32) * inv_scale
    )
    grad_k = (
        jnp.einsum("tqs,tqd->sd", dscore, query_block, preferred_element_type=jnp.float32)
        * inv_scale
    )
    grad_v = jnp.einsum("tqs,tqd->sd", weight_b, cot_block, preferred_element_type=jnp.float32)
    return (attn_full.astype(jnp.bfloat16), grad_q, grad_k, grad_v)


def on_device(embeddings, adapter_down, adapter_up, query_base, key_states, values, grad_out):
    highest = lax.Precision.HIGHEST
    tok_rows = embeddings.shape[0]
    n_ctx = lax.axis_size("ctx")
    total = tok_rows * n_ctx
    group_len = tok_rows * SPAN
    half_group = group_len // 2
    local_kv = key_states.shape[1] // HD
    per_kv = query_base.shape[1] // (local_kv * HD)
    kv_total = local_kv * lax.axis_size("head")
    ctx_index = lax.axis_index("ctx")
    head_base = lax.axis_index("head") * local_kv
    inner = lax.psum(jnp.dot(embeddings, adapter_down, preferred_element_type=jnp.float32), "head")
    up_float = adapter_up.astype(jnp.float32)
    query = (
        query_base.astype(jnp.float32) + 2.0 * jnp.dot(inner, up_float, precision=highest)
    ).astype(jnp.bfloat16)
    stacked = jnp.stack([key_states, values])
    offsets = list(range(-(SPAN - 1), 1))
    nearby = {0: stacked}
    for offset in offsets:
        if offset != 0:
            nearby[offset] = from_behind(stacked, "ctx", -offset)
    key_all = jnp.concatenate([nearby[offset][0] for offset in offsets], axis=0)
    value_all = jnp.concatenate([nearby[offset][1] for offset in offsets], axis=0)
    arange_rows = jnp.arange(tok_rows, dtype=jnp.int32)
    key_pos = jnp.concatenate(
        [(ctx_index + offset) % n_ctx * tok_rows + arange_rows for offset in offsets]
    )
    query_pos = ctx_index * tok_rows + arange_rows
    half_rows = tok_rows // 2
    outs, grad_qs, grad_ks, grad_vs = ([], [], [], [])
    shifted = head_base + 0 >= kv_total // 2
    query_rank = jnp.where(shifted, (query_pos - half_group) % total, query_pos)
    key_rank = jnp.where(shifted, (key_pos - half_group) % total, key_pos)
    allowed = (query_rank[:, None] // group_len == key_rank[None, :] // group_len) & (
        key_rank[None, :] <= query_rank[:, None]
    )
    query_head = query.reshape(2, half_rows, per_kv, HD)
    cot_head = grad_out.reshape(2, half_rows, per_kv, HD)
    mask_head = allowed.reshape(2, half_rows, key_pos.shape[0])
    result = lax.map(
        lambda items: block_pass(items[0], items[1], items[2], key_all, value_all),
        (query_head, cot_head, mask_head),
    )
    outs.append(result[0].reshape(tok_rows, per_kv * HD))
    grad_qs.append(result[1].reshape(tok_rows, per_kv * HD))
    grad_ks.append(jnp.sum(result[2], axis=0))
    grad_vs.append(jnp.sum(result[3], axis=0))
    attn_out = outs[0]
    grad_query = grad_qs[0]
    grad_kv = jnp.stack([grad_ks[0], grad_vs[0]])
    terms = {}
    for position, offset in enumerate(offsets):
        terms[offset] = grad_kv[:, position * tok_rows : (position + 1) * tok_rows]
    received = terms[0]
    for offset in offsets:
        if offset != 0:
            received = received + from_behind(
                terms[offset].astype(jnp.bfloat16), "ctx", offset
            ).astype(jnp.float32)
    grad_inner = lax.psum(2.0 * jnp.dot(grad_query, up_float.T, precision=highest), "head")
    part_up = 2.0 * jnp.dot(inner.T, grad_query, precision=highest)
    part_down = jnp.dot(embeddings.astype(jnp.float32).T, grad_inner, precision=highest)
    grad_adapter_down, grad_adapter_up = lax.psum((part_down, part_up), "ctx")
    grad_embeddings = jnp.dot(grad_inner, adapter_down.astype(jnp.float32).T, precision=highest)
    return (attn_out, grad_embeddings, grad_adapter_down, grad_adapter_up, received[0], received[1])


def solution(mesh):
    in_specs = (
        P("ctx", "head"),
        P("head", None),
        P(None, "head"),
        P("ctx", "head"),
        P("ctx", "head"),
        P("ctx", "head"),
        P("ctx", "head"),
    )
    out_specs = (
        P("ctx", "head"),
        P("ctx", "head"),
        P("head", None),
        P(None, "head"),
        P("ctx", "head"),
        P("ctx", "head"),
    )
    return jax.shard_map(
        on_device, mesh=mesh, in_specs=in_specs, out_specs=out_specs, check_vma=False
    )
```

profile of v0, /device:TPU:1, one launch (start us, length us, event | category | flops | bytes accessed | tf_op | source)
XLA Modules:
  0.0 511.0 jit_solution(14051124300663995487)
XLA Ops:
  8.2 4.6 collective-permute-start.2
  12.8 3.4 collective-permute-start.1
  16.2 2.3 collective-permute-start
  19.6 20.5 %psum.28 = f32[256,8]{0,1:T(8,128)S(1)} all-reduce(f32[256,8]{0,1:T(8,128)S(1)} %fusion.56), channel_id=1, replica_groups=mesh['ctx'=64,'head'=8] {'head'}, use_global_device_ids=true, to_apply=%region_0.0 | all-reduce | flops 2048 | bytes 16384 | tf_op jit(solution)/shard_map/psum | solution.py:56
  40.2 1.7 fusion.30
  42.8 1.9 copy.44
  46.7 39.8 %while.16 = (s32[]{:T(128)}, bf16[2,128,8,128]{3,2,1,0:T(8,128)(2,1)}, f32[2,128,8,128]{3,2,1,0:T(8,128)}, f32[2,1024,128]{2,1,0:T(8,128)}, f32[2,1024,128]{2,1,...) while((s32[]{:T(128)}, ...), condition=%wide.region_5.6_spmd, body=%wide.region_1.5_spmd.sunk | while | flops 1621884928 | bytes 66998552 | solution.py:85
  47.6 1.1 constant_dynamic-slice_fusion.3
  48.9 4.4 fusion.97
  53.4 2.8 fusion.98
  56.2 1.9 multiply_reduce_fusion.2
  58.9 2.2 multiply_convert_fusion.2
  62.1 1.6 fusion.99
  63.7 1.5 fusion.100
  67.5 1.1 constant_dynamic-slice_fusion.3
  68.8 4.4 fusion.97
  73.2 2.8 fusion.98
  76.0 1.9 multiply_reduce_fusion.2
  78.8 2.2 multiply_convert_fusion.2
  82.0 1.6 fusion.99
  83.6 1.5 fusion.100
  86.5 2.0 convolution_multiply_fusion.3
  88.5 2.6 convolution_multiply_fusion.2
  91.1 1.3 reduce_sum.37
  93.4 15.8 %psum.29 = f32[256,8]{0,1:T(8,128)S(1)} all-reduce(f32[256,8]{0,1:T(8,128)S(1)} %convolution_multiply_fusion.3), channel_id=1, replica_groups=mesh['ctx'=64,'head'=8] {'head'}, use_global_device_ids=true, to_apply=%region_6.7 | all-reduce | flops 2048 | bytes 16384 | tf_op jit(solution)/shard_map/psum | solution.py:105
  110.3 15.5 %collective-permute-start.3 = (bf16[2,256,128]{2,1,0:T(8,128)(2,1)S(1)}, bf16[2,256,128]{2,1,0:T(8,128)(2,1)S(1)}, u32[]{:S(2)}, u32[]{:S(2)}) collective-permute-start(bf16[2,256,128]{2,1,0:T(8,128)(2,1)S(1)} %get-tuple-element.115), channel_id=1, source_target_pairs={{24,0},{32,8},{40,16},{48,24},{56,32},{64,40},{72,48},{80,56},{88,... | collective-permute-start | bytes 393224 | tf_op jit(solution)/shard_map/ppermute | solution.py:15
  125.8 1.9 collective-permute-start.5
  127.7 4.2 collective-permute-start.4
  132.0 1.6 fusion.57
  134.7 366.7 %all-reduce.3.cloned.1.call-done = (f32[1024,8]{0,1:T(8,128)}, f32[8,1024]{1,0:T(8,128)}) async-done(((f32[1024,8]{0,1:T(8,128)}, f32[8,1024]{1,0:T(8,128)}), (f32[1024,8]{0,1:T(8,128)}, f32[8,1024]{1,0:T(8,128)})) %all-reduce.3.cloned.1.call-update) | async-done | bytes 65552 | tf_op jit(solution)/shard_map/psum | solution.py:108
  501.4 1.4 copy.101
  502.8 1.4 copy.102
  (77 shorter events, 16.2 us)
Async XLA Ops:
  7.2 11.5 %copy-start = (bf16[256,1024]{1,0:T(8,128)(2,1)S(1)}, bf16[256,1024]{1,0:T(8,128)(2,1)}, u32[]{:S(2)}) copy-start(bf16[256,1024]{1,0:T(8,128)(2,1)} %param.9) | copy-start | bytes 1572868
  7.2 38.7 %copy-start.8 = (bf16[256,128]{1,0:T(8,128)(2,1)S(1)}, bf16[256,128]{1,0:T(8,128)(2,1)}, u32[]{:S(2)}) copy-start(bf16[256,128]{1,0:T(8,128)(2,1)} %param.13) | copy-start | bytes 196612
  7.2 38.7 %copy-start.9 = (bf16[256,128]{1,0:T(8,128)(2,1)S(1)}, bf16[256,128]{1,0:T(8,128)(2,1)}, u32[]{:S(2)}) copy-start(bf16[256,128]{1,0:T(8,128)(2,1)} %param.14) | copy-start | bytes 196612
  7.2 494.2 %all-reduce.3.cloned.1.call-start = ((), (), s32[]{:S(2)}) async-start(), calls=%async_computation | async-start | bytes 131072 | tf_op jit(solution)/shard_map/psum | solution.py:108
  8.2 37.6 %collective-permute-start.2 = (bf16[2,256,128]{2,1,0:T(8,128)(2,1)S(1)}, bf16[2,256,128]{2,1,0:T(8,128)(2,1)S(1)}, u32[]{:S(2)}, u32[]{:S(2)}) collective-permute-start(bf16[2,256,128]{2,1,0:T(8,128)(2,1)S(1)} %pad_maximum_fusion.3), channel_id=1, source_target_pairs={{504,0},{0,8},{8,16},{16,24},{24,32},{32,40},{40,48},{48,56},{56,6... | collective-permute-start | bytes 393224 | tf_op jit(solution)/shard_map/ppermute | solution.py:15
  12.8 33.0 %collective-permute-start.1 = (bf16[2,256,128]{2,1,0:T(8,128)(2,1)S(1)}, bf16[2,256,128]{2,1,0:T(8,128)(2,1)S(1)}, u32[]{:S(2)}, u32[]{:S(2)}) collective-permute-start(bf16[2,256,128]{2,1,0:T(8,128)(2,1)S(1)} %pad_maximum_fusion.3), channel_id=1, source_target_pairs={{496,0},{504,8},{0,16},{8,24},{16,32},{24,40},{32,48},{40,56},{48,... | collective-permute-start | bytes 393224 | tf_op jit(solution)/shard_map/ppermute | solution.py:15
  16.2 29.6 %collective-permute-start = (bf16[2,256,128]{2,1,0:T(8,128)(2,1)S(1)}, bf16[2,256,128]{2,1,0:T(8,128)(2,1)S(1)}, u32[]{:S(2)}, u32[]{:S(2)}) collective-permute-start(bf16[2,256,128]{2,1,0:T(8,128)(2,1)S(1)} %pad_maximum_fusion.3), channel_id=1, source_target_pairs={{488,0},{496,8},{504,16},{0,24},{8,32},{16,40},{24,48},{32,56},{40... | collective-permute-start | bytes 393224 | tf_op jit(solution)/shard_map/ppermute | solution.py:15
  46.7 39.8 %copy-start.10 = (bf16[8,1024]{1,0:T(8,128)(2,1)S(1)}, bf16[8,1024]{1,0:T(8,128)(2,1)}, u32[]{:S(2)}) copy-start(bf16[8,1024]{1,0:T(8,128)(2,1)} %param.11) | copy-start | bytes 49156
  53.4 4.8 copy-start.4
  56.2 2.7 copy-start.1
  58.9 2.3 copy-start.5
  61.3 3.9 copy-start.2
  65.6 1.0 copy-start.3
  73.2 4.8 copy-start.4
  76.0 2.7 copy-start.1
  78.8 2.3 copy-start.5
  81.2 3.9 copy-start.2
  85.5 1.0 copy-start.3
  86.5 5.9 %copy-start.6 = (f32[2,1024,128]{2,1,0:T(8,128)S(1)}, f32[2,1024,128]{2,1,0:T(8,128)}, u32[]{:S(2)}) copy-start(f32[2,1024,128]{2,1,0:T(8,128)} %get-tuple-element.63) | copy-start | bytes 3145732
  86.5 6.1 %copy-start.7 = (bf16[2,128,8,128]{3,2,1,0:T(8,128)(2,1)S(1)}, bf16[2,128,8,128]{3,2,1,0:T(8,128)(2,1)}, u32[]{:S(2)}) copy-start(bf16[2,128,8,128]{3,2,1,0:T(8,128)(2,1)} %get-tuple-element.61) | copy-start | bytes 1572868
  88.5 43.5 %copy-start.11 = (bf16[1024,8]{0,1:T(8,128)(2,1)S(1)}, bf16[1024,8]{0,1:T(8,128)(2,1)}, u32[]{:S(2)}) copy-start(bf16[1024,8]{0,1:T(8,128)(2,1)} %param.10) | copy-start | bytes 49156
  110.3 23.3 %collective-permute-start.3 = (bf16[2,256,128]{2,1,0:T(8,128)(2,1)S(1)}, bf16[2,256,128]{2,1,0:T(8,128)(2,1)S(1)}, u32[]{:S(2)}, u32[]{:S(2)}) collective-permute-start(bf16[2,256,128]{2,1,0:T(8,128)(2,1)S(1)} %get-tuple-element.115), channel_id=1, source_target_pairs={{24,0},{32,8},{40,16},{48,24},{56,32},{64,40},{72,48},{80,56},{88,... | collective-permute-start | bytes 393224 | tf_op jit(solution)/shard_map/ppermute | solution.py:15
  125.8 7.8 %collective-permute-start.5 = (bf16[2,256,128]{2,1,0:T(8,128)(2,1)S(1)}, bf16[2,256,128]{2,1,0:T(8,128)(2,1)S(1)}, u32[]{:S(2)}, u32[]{:S(2)}) collective-permute-start(bf16[2,256,128]{2,1,0:T(8,128)(2,1)S(1)} %get-tuple-element.116), channel_id=1, source_target_pairs={{8,0},{16,8},{24,16},{32,24},{40,32},{48,40},{56,48},{64,56},{72,6... | collective-permute-start | bytes 393224 | tf_op jit(solution)/shard_map/ppermute | solution.py:15
  127.7 6.2 %collective-permute-start.4 = (bf16[2,256,128]{2,1,0:T(8,128)(2,1)S(1)}, bf16[2,256,128]{2,1,0:T(8,128)(2,1)S(1)}, u32[]{:S(2)}, u32[]{:S(2)}) collective-permute-start(bf16[2,256,128]{2,1,0:T(8,128)(2,1)S(1)} %get-tuple-element.117), channel_id=1, source_target_pairs={{16,0},{24,8},{32,16},{40,24},{48,32},{56,40},{64,48},{72,56},{80,... | collective-permute-start | bytes 393224 | tf_op jit(solution)/shard_map/ppermute | solution.py:15
Sparse Core Ops, SparseCore 0:
  132.1 369.2 all-reduce.2
where the time goes:
time: 512 us; the launch traced here: 511 us
  waiting for transfers between devices  367 us (72%)
  blocking collectives  36.3 us (7%)
  matrix products  34.8 us (7%)
  starting transfers between devices  32 us (6%)
  local copies, waits for them, and re-layouts  16.2 us (3%)
  between operations  14.4 us (3%)
  other arithmetic  9.95 us (2%)
    psum x1, waiting for transfers between devices, on_device(): grad_adapter_down, grad_adapter_up = lax.psum((part_down, part_up), 'ctx')  367 us
    ppermute x6, starting transfers between devices, from_behind(): return lax.ppermute(block, axis, route)  32 us
    psum x1, blocking collectives, on_device(): lax.psum(jnp.dot(embeddings, adapter_down, preferred_element_type=jnp.flo...  20.5 us
    psum x1, blocking collectives, on_device(): lax.psum(2.0 * jnp.dot(grad_query, up_float.T, precision=highest), 'head')  15.8 us
  transfers between devices with their start and end apart: 7, of which 2 were waited for; matrix products, arithmetic and copies ran while one was open for 2% of the time, Pallas kernels for 0%

commit v1 on v0

v1 whole, which is shorter than its diff:
```python
import functools
import math

import jax
import jax.numpy as jnp
from jax import lax
from jax.experimental import pallas as pl
from jax.experimental.pallas import tpu as pltpu
from jax.sharding import PartitionSpec as P

HD = 128
SPAN = 4
FAR = 1e30
F32 = jnp.float32
BF16 = jnp.bfloat16
NT = (((1,), (1,)), ((), ()))
TN = (((0,), (0,)), ((), ()))
MAIN_VMEM = 40 * 2**20
SMALL_VMEM = 16 * 2**20


def dot(a, b, dims=(((1,), (0,)), ((), ()))):
    return lax.dot_general(a, b, dims, preferred_element_type=F32)


def split3(x):
    hi = x.astype(BF16).astype(F32)
    rest = x - hi
    mid = rest.astype(BF16).astype(F32)
    low = rest - mid
    return jnp.concatenate([hi, mid, low, jnp.zeros_like(x)], axis=0).astype(BF16)


def thrice(x):
    x = x.astype(F32)
    return jnp.concatenate([x, x, x, jnp.zeros_like(x)], axis=0).astype(BF16)


def first_kernel(emb_ref, down_ref, key_ref, value_ref, parts_ref, kv_ref):
    part = dot(down_ref[...], emb_ref[...], NT)
    for peer in range(parts_ref.shape[0]):
        parts_ref[peer] = part
    kv_ref[0] = key_ref[...]
    kv_ref[1] = value_ref[...]


def main_kernel(
    heads_per_step,
    parts_ref,
    up_ref,
    base_ref,
    cot_ref,
    own_ref,
    near_ref,
    mid_ref,
    far_ref,
    attn_ref,
    inner_parts_ref,
    part_up_ref,
    grad_own_ref,
    grad_near_ref,
    grad_mid_ref,
    grad_far_ref,
    query_ref,
    key_ref,
    value_ref,
    key_t_ref,
    value_t_ref,
    grad_q_ref,
    acc_k_ref,
    acc_v_ref,
):
    rows = base_ref.shape[0]
    heads = base_ref.shape[1] // HD
    inv_scale = 1.0 / math.sqrt(HD)
    to_exp2 = inv_scale * math.log2(math.e)
    n_head = lax.axis_size("head")
    shift = jnp.where(lax.axis_index("head") >= n_head // 2, SPAN // 2, 0)
    rank = lax.rem(lax.axis_index("ctx") + SPAN - shift, SPAN)

    inner = jnp.sum(parts_ref[...], axis=0)
    inner3 = split3(inner)
    query_ref[...] = (
        base_ref[...].astype(F32) + 2.0 * dot(inner3, thrice(up_ref[...]), TN)
    ).astype(BF16)
    for position, ref in enumerate((far_ref, mid_ref, near_ref, own_ref)):
        at = slice(position * rows, (position + 1) * rows)
        key_ref[at, :] = ref[0]
        value_ref[at, :] = ref[1]
        key_t_ref[:, at] = ref[0].astype(F32).T.astype(BF16)
        value_t_ref[:, at] = ref[1].astype(F32).T.astype(BF16)
    acc_k_ref[...] = jnp.zeros_like(acc_k_ref)
    acc_v_ref[...] = jnp.zeros_like(acc_v_ref)

    source = lax.broadcasted_iota(jnp.int32, (rows, rows), 0)
    target = lax.broadcasted_iota(jnp.int32, (rows, rows), 1)
    causal = source <= target
    closed = [jnp.where(rank >= SPAN - 1 - p, 0.0, FAR) for p in range(SPAN - 1)]

    def one_head(head):
        at = pl.ds(pl.multiple_of(head * HD, HD), HD)
        query, cot = query_ref[:, at], cot_ref[:, at]
        scores = dot(key_ref[...], query, NT)
        blocks = [scores[p * rows : (p + 1) * rows] for p in range(SPAN)]
        blocks[-1] = jnp.where(causal, blocks[-1], -FAR)
        tops = [jnp.max(block, axis=0, keepdims=True) for block in blocks]
        top = tops[-1]
        for p in range(SPAN - 1):
            top = jnp.maximum(top, tops[p] - closed[p])
        limits = [top + closed[p] for p in range(SPAN - 1)] + [top]
        powers = [jnp.exp2((b - t) * to_exp2) for b, t in zip(blocks, limits)]
        total = sum(jnp.sum(power, axis=0, keepdims=True) for power in powers)
        weight = jnp.concatenate(powers, axis=0) * (1.0 / total)
        weight_b = weight.astype(BF16)
        attn_t = dot(value_t_ref[...], weight_b)
        cot_t = cot.astype(F32).T
        delta = jnp.sum(cot_t * attn_t, axis=0, keepdims=True)
        attn_ref[:, at] = attn_t.T.astype(BF16)
        dprob = dot(value_ref[...], cot, NT)
        dscore = (weight * (dprob - delta)).astype(BF16)
        grad_q_ref[at, :] = dot(key_t_ref[...], dscore) * (2.0 * inv_scale)
        return query, cot, weight_b, dscore

    def step(i, carry):
        got = [one_head(i * heads_per_step + j) for j in range(heads_per_step)]
        query, cot = (jnp.concatenate([g[k] for g in got], axis=0) for k in (0, 1))
        weight_b, dscore = (jnp.concatenate([g[k] for g in got], axis=1) for k in (2, 3))
        acc_v_ref[...] += dot(weight_b, cot)
        acc_k_ref[...] += dot(dscore, query)
        return carry

    lax.fori_loop(0, heads // heads_per_step, step, 0)

    outs = (grad_far_ref, grad_mid_ref, grad_near_ref, grad_own_ref)
    for position, ref in enumerate(outs):
        at = slice(position * rows, (position + 1) * rows)
        ref[0] = (acc_k_ref[at, :] * inv_scale).astype(ref.dtype)
        ref[1] = acc_v_ref[at, :].astype(ref.dtype)

    grad_q = grad_q_ref[...]
    high = grad_q.astype(BF16)
    low = (grad_q - high.astype(F32)).astype(BF16)
    up = up_ref[...]
    grad_inner = dot(up, high) + dot(up, low)
    for peer in range(inner_parts_ref.shape[0]):
        inner_parts_ref[peer] = grad_inner
    r = inner.shape[0]
    rows3 = dot(inner3, high, NT)
    part_up = rows3[:r] + rows3[r : 2 * r] + rows3[2 * r : 3 * r]
    rows3 = dot(inner3, low, NT)
    part_up_ref[...] = part_up + rows3[:r] + rows3[r : 2 * r]


def last_kernel(parts_ref, emb_ref, down_ref, part_up_ref, grad_emb_ref, pieces_ref):
    grad_inner = jnp.sum(parts_ref[...], axis=0)
    r = grad_inner.shape[0]
    terms = split3(grad_inner)
    rows3 = dot(terms, emb_ref[...])
    part_down = rows3[:r] + rows3[r : 2 * r] + rows3[2 * r : 3 * r]
    grad_emb_ref[...] = dot(terms, thrice(down_ref[...]), TN)
    half = pieces_ref.shape[0] // 2
    width = pieces_ref.shape[2]
    for piece in range(half):
        at = slice(piece * width, (piece + 1) * width)
        pieces_ref[piece] = part_down[:, at]
        pieces_ref[half + piece] = part_up_ref[:, at]


def call(kernel, outs, *args, scratch=(), limit=SMALL_VMEM, name=None):
    return pl.pallas_call(
        kernel,
        out_shape=[jax.ShapeDtypeStruct(shape, dtype) for shape, dtype in outs],
        scratch_shapes=scratch,
        compiler_params=pltpu.CompilerParams(vmem_limit_bytes=limit),
        name=name,
    )(*args)


def ctx_groups(n_ctx, n_head, members):
    return [[c * n_head + h for c in group] for group in members for h in range(n_head)]


def on_device(embeddings, adapter_down, adapter_up, query_base, key_states, values, grad_out):
    rows, width = query_base.shape
    r = adapter_up.shape[0]
    n_ctx, n_head = lax.axis_size("ctx"), lax.axis_size("head")
    both = ("ctx", "head")
    keys = SPAN * rows
    down_t = adapter_down.T

    def route(distance, back=False):
        pairs = []
        for head in range(n_head):
            shift = SPAN // 2 if head >= n_head // 2 else 0
            for ctx in range(n_ctx):
                if (ctx - shift) % SPAN + distance < SPAN:
                    pair = (ctx * n_head + head, (ctx + distance) % n_ctx * n_head + head)
                    pairs.append(pair[::-1] if back else pair)
        return pairs

    parts, kv = call(
        first_kernel,
        [((n_head, r, rows), F32), ((2, rows, HD), BF16)],
        embeddings,
        down_t,
        key_states,
        values,
        name="inner_parts",
    )
    near, mid, far = (lax.ppermute(kv, both, route(d)) for d in (1, 2, 3))
    parts = lax.all_to_all(parts, "head", 0, 0)
    attn_out, inner_parts, part_up, grad_own, grad_near, grad_mid, grad_far = call(
        functools.partial(main_kernel, 2),
        [
            ((rows, width), BF16),
            ((n_head, r, rows), F32),
            ((r, width), F32),
            ((2, rows, HD), F32),
            ((2, rows, HD), BF16),
            ((2, rows, HD), BF16),
            ((2, rows, HD), BF16),
        ],
        parts,
        adapter_up,
        query_base,
        grad_out,
        kv,
        near,
        mid,
        far,
        scratch=[
            pltpu.VMEM((rows, width), BF16),
            pltpu.VMEM((keys, HD), BF16),
            pltpu.VMEM((keys, HD), BF16),
            pltpu.VMEM((HD, keys), BF16),
            pltpu.VMEM((HD, keys), BF16),
            pltpu.VMEM((width, rows), F32),
            pltpu.VMEM((keys, HD), F32),
            pltpu.VMEM((keys, HD), F32),
        ],
        limit=MAIN_VMEM,
        name="attention",
    )
    sent = [
        lax.ppermute(term, both, route(d, back=True))
        for d, term in ((1, grad_near), (2, grad_mid), (3, grad_far))
    ]
    inner_parts = lax.all_to_all(inner_parts, "head", 0, 0)

    wide = 16
    close = [[g * wide + m for m in range(wide)] for g in range(n_ctx // wide)]
    apart = [[g * wide + m for g in range(n_ctx // wide)] for m in range(wide)]
    close, apart = (ctx_groups(n_ctx, n_head, groups) for groups in (close, apart))
    piece = 2 * width // wide
    grad_embeddings, pieces = call(
        last_kernel,
        [((rows, width), F32), ((wide, r, piece), F32)],
        inner_parts,
        embeddings,
        down_t,
        part_up,
        name="grad_embeddings",
    )
    pieces = lax.all_to_all(pieces, both, 0, 0, axis_index_groups=close)
    mine = jnp.sum(pieces, axis=0)
    mine = jnp.broadcast_to(mine[None], (n_ctx // wide, *mine.shape))
    mine = lax.all_to_all(mine, both, 0, 0, axis_index_groups=apart)
    mine = jnp.sum(mine, axis=0)
    mine = jnp.broadcast_to(mine[None], (wide, *mine.shape))
    whole = lax.all_to_all(mine, both, 0, 0, axis_index_groups=close)
    whole = whole.transpose(1, 0, 2).reshape(r, 2 * width)
    grad_adapter_down, grad_adapter_up = whole[:, :width].T, whole[:, width:]

    received = grad_own
    for term in sent:
        received = received + term.astype(F32)
    return (
        attn_out,
        grad_embeddings,
        grad_adapter_down,
        grad_adapter_up,
        received[0],
        received[1],
    )


def solution(mesh):
    in_specs = (
        P("ctx", "head"),
        P("head", None),
        P(None, "head"),
        P("ctx", "head"),
        P("ctx", "head"),
        P("ctx", "head"),
        P("ctx", "head"),
    )
    out_specs = (
        P("ctx", "head"),
        P("ctx", "head"),
        P("head", None),
        P(None, "head"),
        P("ctx", "head"),
        P("ctx", "head"),
    )
    return jax.shard_map(
        on_device, mesh=mesh, in_specs=in_specs, out_specs=out_specs, check_vma=False
    )
```

time: 512 us -> 102 us (0.20)
  waiting for transfers between devices: 367 us -> 7.3 us
  matrix products: 34.8 us -> 0 us
  Pallas kernels: 0 us -> 14.9 us
  between operations: 14.4 us -> 0.77 us
  other arithmetic: 9.95 us -> 0.08 us
  local copies, waits for them, and re-layouts: 16.2 us -> 6.53 us
  blocking collectives: 36.3 us -> 44 us
    psum x1 -> x0, waiting for transfers between devices: 367 us -> none  [on_device(): grad_adapter_down, grad_adapter_up = lax.psum((part_down, part_up), 'ctx')]
    all_to_all x0 -> x3, blocking collectives: none -> 44 us  [the longest x1 21.2 us: on_device(): mine = lax.all_to_all(mine, both, 0, 0, axis_index_groups=apart)]
    psum x2 -> x0, blocking collectives: 36.3 us -> none  [the longest x1 20.5 us: on_device(): lax.psum(jnp.dot(embeddings, adapter_down, preferred_element_type=jnp.flo...]
    dot_general x16 -> x0, matrix products: 26 us -> none  [the longest x2 4.47 us: block_pass(): jnp.einsum('tqd,sd->tqs', cot_block, value_head, preferred_element_type=j...]
    ppermute x6, starting transfers between devices: 32 us -> 11.2 us  [the longest x3 7.27 us: on_device(): near, mid, far = (lax.ppermute(kv, both, route(d)) for d in (1, 2, 3))]
    all_to_all x0 -> x2, starting transfers between devices: none -> 16.2 us  [the longest x1 10.4 us: on_device(): pieces = lax.all_to_all(pieces, both, 0, 0, axis_index_groups=close)]
    pallas_call x0 -> x3, Pallas kernels: none -> 14.9 us  [call(): pl.pallas_call(kernel, out_shape=[jax.ShapeDtypeStruct(shape, dtype) for...]
    sub x2 -> x0, matrix products: 8.81 us -> none  [block_pass(): weight = jnp.exp(scores - top)]
  transfers between devices with their start and end apart: 7 -> 8, of which waited for: 2 -> 2; matrix products, arithmetic and copies ran while one was open for 2% -> 1% of each run, Pallas kernels for 0% -> 0%
where the time goes in v1:
time: 102 us; the launch traced here: 101 us
  blocking collectives  44 us (43%)
  starting transfers between devices  27.5 us (27%)
  Pallas kernels  14.9 us (15%)
  waiting for transfers between devices  7.3 us (7%)
  local copies, waits for them, and re-layouts  6.53 us (6%)
    all_to_all x1, blocking collectives, on_device(): mine = lax.all_to_all(mine, both, 0, 0, axis_index_groups=apart)  21.2 us
    pallas_call x3, Pallas kernels, call(): pl.pallas_call(kernel, out_shape=[jax.ShapeDtypeStruct(shape, dtype) for...  14.9 us
    all_to_all x1, blocking collectives, on_device(): inner_parts = lax.all_to_all(inner_parts, 'head', 0, 0)  11.5 us
    all_to_all x1, blocking collectives, on_device(): parts = lax.all_to_all(parts, 'head', 0, 0)  11.2 us
    all_to_all x1, starting transfers between devices, on_device(): pieces = lax.all_to_all(pieces, both, 0, 0, axis_index_groups=close)  10.4 us
    ppermute x3, starting transfers between devices, on_device(): near, mid, far = (lax.ppermute(kv, both, route(d)) for d in (1, 2, 3))  7.27 us
    all_to_all x1, starting transfers between devices, on_device(): whole = lax.all_to_all(mine, both, 0, 0, axis_index_groups=close)  5.87 us
    all_to_all x1, waiting for transfers between devices, on_device(): whole = lax.all_to_all(mine, both, 0, 0, axis_index_groups=close)  5.23 us
  transfers between devices with their start and end apart: 8, of which 2 were waited for; matrix products, arithmetic and copies ran while one was open for 1% of the time, Pallas kernels for 0%

profile of v1, /device:TPU:1, one launch (start us, length us, event | category | flops | bytes accessed | tf_op | source)
XLA Modules:
  0.0 101.1 jit_solution(5975513964516054793)
XLA Ops:
  0.6 0.0 copy-start
  0.6 1.0 %copy-done = bf16[256,1024]{1,0:T(8,128)(2,1)S(1)} copy-done((bf16[256,1024]{1,0:T(8,128)(2,1)S(1)}, bf16[256,1024]{1,0:T(8,128)(2,1)}, u32[]{:S(2)}) %copy-start) | copy-done | bytes 524312
  1.7 0.8 copy-done.4
  2.5 0.8 copy-done.5
  3.4 0.7 copy-done.6
  4.1 0.2 inner_parts.1
  4.3 0.7 collective-permute-start.2
  5.0 4.7 %collective-permute-start.1 = (bf16[2,256,128]{2,1,0:T(8,128)(2,1)S(1)}, bf16[2,256,128]{2,1,0:T(8,128)(2,1)S(1)}, u32[]{:S(2)}, u32[]{:S(2)}) collective-permute-start(bf16[2,256,128]{2,1,0:T(8,128)(2,1)S(1)} %get-tuple-element.18.own_ref), channel_id=1, source_target_pairs={{0,16},{8,24},{32,48},{40,56},{64,80},{72,88},{96,112},{104,120},{... | collective-permute-start | bytes 393224 | tf_op jit(solution)/shard_map/ppermute | solution.py:210
  9.7 1.9 %collective-permute-start = (bf16[2,256,128]{2,1,0:T(8,128)(2,1)S(1)}, bf16[2,256,128]{2,1,0:T(8,128)(2,1)S(1)}, u32[]{:S(2)}, u32[]{:S(2)}) collective-permute-start(bf16[2,256,128]{2,1,0:T(8,128)(2,1)S(1)} %get-tuple-element.18.own_ref), channel_id=1, source_target_pairs={{0,8},{8,16},{16,24},{32,40},{40,48},{48,56},{64,72},{72,80},{80,8... | collective-permute-start | bytes 393224 | tf_op jit(solution)/shard_map/ppermute | solution.py:210
  11.6 0.0 copy-start.8
  11.6 11.2 %all_to_all.25.parts_ref = f32[8,8,256]{2,1,0:T(8,128)S(1)} all-to-all(f32[8,8,256]{2,1,0:T(8,128)S(1)} %get-tuple-element.17), channel_id=1, replica_groups=mesh['ctx'=64,'head'=8] {'head'}, dimensions={0} | all-to-all | bytes 131072 | tf_op jit(solution)/shard_map/all_to_all | solution.py:211
  22.8 0.0 collective-permute-done.2.far_ref
  22.8 0.0 collective-permute-done.1.mid_ref
  22.9 0.0 collective-permute-done.near_ref
  22.9 0.0 copy-start.3
  22.9 1.1 %copy-done.3 = bf16[256,1024]{1,0:T(8,128)(2,1)S(1)} copy-done((bf16[256,1024]{1,0:T(8,128)(2,1)S(1)}, bf16[256,1024]{1,0:T(8,128)(2,1)}, u32[]{:S(2)}) %copy-start.3) | copy-done | bytes 524312
  24.0 13.4 %attention.1 = (bf16[256,1024]{1,0:T(8,128)(2,1)}, f32[8,8,256]{2,1,0:T(8,128)S(1)}, f32[8,1024]{1,0:T(8,128)S(1)}, f32[2,256,128]{2,1,0:T(8,128)S(1)}, bf16[2,2...) custom-call(f32[8,8,256]{2,1,0:T(8,128)S(1)} %all_to_all.25.parts_ref, ...), custom_call_target="tpu_custom_call" | custom-call | tf_op jit(solution)/shard_map/attention/pallas_call | solution.py:170
  37.4 11.5 %all_to_all.26.parts_ref = f32[8,8,256]{2,1,0:T(8,128)S(1)} all-to-all(f32[8,8,256]{2,1,0:T(8,128)S(1)} %get-tuple-element.20), channel_id=1, replica_groups=mesh['ctx'=64,'head'=8] {'head'}, dimensions={0} | all-to-all | bytes 131072 | tf_op jit(solution)/shard_map/all_to_all | solution.py:248
  48.9 1.3 %grad_embeddings.1 = (f32[256,1024]{1,0:T(8,128)}, f32[16,8,128]{2,1,0:T(8,128)}) custom-call(f32[8,8,256]{2,1,0:T(8,128)S(1)} %all_to_all.26.parts_ref, bf16[256,1024]{1,0:T(8,128)(2,1)S(1)} %copy-done.1, bf16[8,1024]{1,0:T(8,128)(2,1)S(1)} %bitcast.11, f32[8,1024]{1,0:T(8,128)S(1)} %get-tuple-element.21.part_up_ref), custom_call_target="tpu_custom_call" | custom-call | tf_op jit(solution)/shard_map/grad_embeddings/pallas_call | solution.py:170
  50.2 10.4 %all-to-all-start.2 = ((f32[16,8,128]{2,1,0:T(8,128)}), f32[16,8,128]{2,1,0:T(8,128)S(1)}, u32[]{:S(2)}, u32[]{:S(2)}) async-start(f32[16,8,128]{2,1,0:T(8,128)} %get-tuple-element.23), calls=%async_computation.2 | async-start | bytes 131072 | tf_op jit(solution)/shard_map/all_to_all | solution.py:264
  60.6 2.0 %collective-permute-start.3 = (bf16[2,256,128]{2,1,0:T(8,128)(2,1)S(1)}, bf16[2,256,128]{2,1,0:T(8,128)(2,1)S(1)}, u32[]{:S(2)}, u32[]{:S(2)}) collective-permute-start(bf16[2,256,128]{2,1,0:T(8,128)(2,1)S(1)} %get-tuple-element.25), channel_id=1, source_target_pairs={{8,0},{16,8},{24,16},{40,32},{48,40},{56,48},{72,64},{80,72},{88,8... | collective-permute-start | bytes 393224 | tf_op jit(solution)/shard_map/ppermute | solution.py:245
  62.6 1.3 %collective-permute-start.4 = (bf16[2,256,128]{2,1,0:T(8,128)(2,1)S(1)}, bf16[2,256,128]{2,1,0:T(8,128)(2,1)S(1)}, u32[]{:S(2)}, u32[]{:S(2)}) collective-permute-start(bf16[2,256,128]{2,1,0:T(8,128)(2,1)S(1)} %get-tuple-element.26), channel_id=1, source_target_pairs={{16,0},{24,8},{48,32},{56,40},{80,64},{88,72},{112,96},{120,104},{... | collective-permute-start | bytes 393224 | tf_op jit(solution)/shard_map/ppermute | solution.py:245
  63.9 0.7 collective-permute-start.5
  64.6 2.1 %all-to-all-done.2 = f32[16,8,128]{2,1,0:T(8,128)S(1)} async-done(((f32[16,8,128]{2,1,0:T(8,128)}), f32[16,8,128]{2,1,0:T(8,128)S(1)}, u32[]{:S(2)}, u32[]{:S(2)}) %all-to-all-start.2) | async-done | bytes 65568 | tf_op jit(solution)/shard_map/all_to_all | solution.py:264
  66.7 21.2 %all_to_all.27 = f32[4,8,128]{2,1,0:T(8,128)S(1)} all-to-all(f32[4,8,128]{2,1,0:T(8,128)S(1)} %broadcast_in_dim.4), channel_id=1, replica_groups={{0,128,256,384},{1,129,257,385},{2,130,258,386},{3,131,259,387},{4,132,..., dimensions={0} | all-to-all | bytes 32768 | tf_op jit(solution)/shard_map/all_to_all | solution.py:267
  87.9 0.6 broadcast_in_dim.5
  88.6 5.9 %all-to-all-start.4 = ((f32[16,8,128]{2,1,0:T(8,128)}), f32[16,8,128]{2,1,0:T(8,128)S(1)}, u32[]{:S(2)}, u32[]{:S(2)}) async-start(f32[16,8,128]{2,1,0:T(8,128)} %broadcast_in_dim.5), calls=%async_computation.4 | async-start | bytes 131072 | tf_op jit(solution)/shard_map/all_to_all | solution.py:270
  94.4 0.0 collective-permute-done.4
  94.5 0.1 convert_add_fusion
  94.5 0.7 slice_bitcast_fusion
  95.2 5.2 %all-to-all-done.4 = f32[16,8,128]{2,1,0:T(8,128)S(1)} async-done(((f32[16,8,128]{2,1,0:T(8,128)}), f32[16,8,128]{2,1,0:T(8,128)S(1)}, u32[]{:S(2)}, u32[]{:S(2)}) %all-to-all-start.4) | async-done | bytes 65568 | tf_op jit(solution)/shard_map/all_to_all | solution.py:270
  100.5 0.6 fusion
  (15 shorter events, 0.1 us)
Async XLA Ops:
  0.6 1.0 %copy-start = (bf16[256,1024]{1,0:T(8,128)(2,1)S(1)}, bf16[256,1024]{1,0:T(8,128)(2,1)}, u32[]{:S(2)}) copy-start(bf16[256,1024]{1,0:T(8,128)(2,1)} %emb_ref.3) | copy-start | bytes 1572868
  1.7 0.8 copy-start.4
  2.5 0.8 copy-start.5
  3.4 0.7 copy-start.6
  4.1 18.8 %copy-start.2 = (bf16[256,1024]{1,0:T(8,128)(2,1)S(1)}, bf16[256,1024]{1,0:T(8,128)(2,1)}, u32[]{:S(2)}) copy-start(bf16[256,1024]{1,0:T(8,128)(2,1)} %base_ref.1) | copy-start | bytes 1572868
  4.3 18.5 %collective-permute-start.2 = (bf16[2,256,128]{2,1,0:T(8,128)(2,1)S(1)}, bf16[2,256,128]{2,1,0:T(8,128)(2,1)S(1)}, u32[]{:S(2)}, u32[]{:S(2)}) collective-permute-start(bf16[2,256,128]{2,1,0:T(8,128)(2,1)S(1)} %get-tuple-element.18.own_ref), channel_id=1, source_target_pairs={{0,24},{32,56},{64,88},{96,120},{128,152},{160,184},{192,216},{224... | collective-permute-start | bytes 393224 | tf_op jit(solution)/shard_map/ppermute | solution.py:210
  5.0 17.9 %collective-permute-start.1 = (bf16[2,256,128]{2,1,0:T(8,128)(2,1)S(1)}, bf16[2,256,128]{2,1,0:T(8,128)(2,1)S(1)}, u32[]{:S(2)}, u32[]{:S(2)}) collective-permute-start(bf16[2,256,128]{2,1,0:T(8,128)(2,1)S(1)} %get-tuple-element.18.own_ref), channel_id=1, source_target_pairs={{0,16},{8,24},{32,48},{40,56},{64,80},{72,88},{96,112},{104,120},{... | collective-permute-start | bytes 393224 | tf_op jit(solution)/shard_map/ppermute | solution.py:210
  9.7 13.2 %collective-permute-start = (bf16[2,256,128]{2,1,0:T(8,128)(2,1)S(1)}, bf16[2,256,128]{2,1,0:T(8,128)(2,1)S(1)}, u32[]{:S(2)}, u32[]{:S(2)}) collective-permute-start(bf16[2,256,128]{2,1,0:T(8,128)(2,1)S(1)} %get-tuple-element.18.own_ref), channel_id=1, source_target_pairs={{0,8},{8,16},{16,24},{32,40},{40,48},{48,56},{64,72},{72,80},{80,8... | collective-permute-start | bytes 393224 | tf_op jit(solution)/shard_map/ppermute | solution.py:210
  11.6 11.3 %copy-start.8 = (bf16[8,1024]{1,0:T(8,128)(2,1)S(1)}, bf16[8,1024]{1,0:T(8,128)(2,1)}, u32[]{:S(2)}) copy-start(bf16[8,1024]{1,0:T(8,128)(2,1)} %up_ref.1) | copy-start | bytes 49156
  22.8 26.1 %copy-start.1 = (bf16[256,1024]{1,0:T(8,128)(2,1)S(1)}, bf16[256,1024]{1,0:T(8,128)(2,1)}, u32[]{:S(2)}) copy-start(bf16[256,1024]{1,0:T(8,128)(2,1)} %emb_ref.3) | copy-start | bytes 1572868
  22.9 1.1 %copy-start.3 = (bf16[256,1024]{1,0:T(8,128)(2,1)S(1)}, bf16[256,1024]{1,0:T(8,128)(2,1)}, u32[]{:S(2)}) copy-start(bf16[256,1024]{1,0:T(8,128)(2,1)} %cot_ref.1) | copy-start | bytes 1572868
  37.4 11.5 %copy-start.7 = (bf16[1024,8]{0,1:T(8,128)(2,1)S(1)}, bf16[1024,8]{0,1:T(8,128)(2,1)}, u32[]{:S(2)}) copy-start(bf16[1024,8]{0,1:T(8,128)(2,1)} %param.8) | copy-start | bytes 49156
  50.2 16.4 %all-to-all-start.2 = ((f32[16,8,128]{2,1,0:T(8,128)}), f32[16,8,128]{2,1,0:T(8,128)S(1)}, u32[]{:S(2)}, u32[]{:S(2)}) async-start(f32[16,8,128]{2,1,0:T(8,128)} %get-tuple-element.23), calls=%async_computation.2 | async-start | bytes 131072 | tf_op jit(solution)/shard_map/all_to_all | solution.py:264
  60.6 33.8 %collective-permute-start.3 = (bf16[2,256,128]{2,1,0:T(8,128)(2,1)S(1)}, bf16[2,256,128]{2,1,0:T(8,128)(2,1)S(1)}, u32[]{:S(2)}, u32[]{:S(2)}) collective-permute-start(bf16[2,256,128]{2,1,0:T(8,128)(2,1)S(1)} %get-tuple-element.25), channel_id=1, source_target_pairs={{8,0},{16,8},{24,16},{40,32},{48,40},{56,48},{72,64},{80,72},{88,8... | collective-permute-start | bytes 393224 | tf_op jit(solution)/shard_map/ppermute | solution.py:245
  62.6 31.8 %collective-permute-start.4 = (bf16[2,256,128]{2,1,0:T(8,128)(2,1)S(1)}, bf16[2,256,128]{2,1,0:T(8,128)(2,1)S(1)}, u32[]{:S(2)}, u32[]{:S(2)}) collective-permute-start(bf16[2,256,128]{2,1,0:T(8,128)(2,1)S(1)} %get-tuple-element.26), channel_id=1, source_target_pairs={{16,0},{24,8},{48,32},{56,40},{80,64},{88,72},{112,96},{120,104},{... | collective-permute-start | bytes 393224 | tf_op jit(solution)/shard_map/ppermute | solution.py:245
  63.9 30.5 %collective-permute-start.5 = (bf16[2,256,128]{2,1,0:T(8,128)(2,1)S(1)}, bf16[2,256,128]{2,1,0:T(8,128)(2,1)S(1)}, u32[]{:S(2)}, u32[]{:S(2)}) collective-permute-start(bf16[2,256,128]{2,1,0:T(8,128)(2,1)S(1)} %get-tuple-element.27), channel_id=1, source_target_pairs={{24,0},{56,32},{88,64},{120,96},{152,128},{184,160},{216,192},{248... | collective-permute-start | bytes 393224 | tf_op jit(solution)/shard_map/ppermute | solution.py:245
  88.6 11.9 %all-to-all-start.4 = ((f32[16,8,128]{2,1,0:T(8,128)}), f32[16,8,128]{2,1,0:T(8,128)S(1)}, u32[]{:S(2)}, u32[]{:S(2)}) async-start(f32[16,8,128]{2,1,0:T(8,128)} %broadcast_in_dim.5), calls=%async_computation.4 | async-start | bytes 131072 | tf_op jit(solution)/shard_map/all_to_all | solution.py:270

commit v2 on v1

v2 whole, which is shorter than its diff:
```python
import functools
import math

import jax
import jax.numpy as jnp
from jax import lax
from jax.experimental import pallas as pl
from jax.experimental.pallas import tpu as pltpu
from jax.sharding import PartitionSpec as P

HD = 128
TIE = 0
HPS = 4
RM = 2
RH = 5
FIRST_LOW = 12
FIRST_HIGH = 0
TURN = 8
WIDE_BACK = False
SENT = jnp.float32
FIRST_VMEM = 16 * 2**20
SPAN = 4
FAR = 1e30
F32 = jnp.float32
BF16 = jnp.bfloat16
NT = (((1,), (1,)), ((), ()))
TN = (((0,), (0,)), ((), ()))
MAIN_VMEM = 40 * 2**20
SMALL_VMEM = 16 * 2**20


def dot(a, b, dims=(((1,), (0,)), ((), ()))):
    return lax.dot_general(a, b, dims, preferred_element_type=F32)


def split3(x):
    hi = x.astype(BF16).astype(F32)
    rest = x - hi
    mid = rest.astype(BF16).astype(F32)
    low = rest - mid
    return jnp.concatenate([hi, mid, low, jnp.zeros_like(x)], axis=0).astype(BF16)


def thrice(x):
    x = x.astype(F32)
    return jnp.concatenate([x, x, x, jnp.zeros_like(x)], axis=0).astype(BF16)


def first_kernel(emb_hbm, down_hbm, parts_ref, emb_ref, down_ref, sems):
    copies = [
        pltpu.make_async_copy(down_hbm, down_ref, sems.at[0]),
        pltpu.make_async_copy(emb_hbm, emb_ref, sems.at[1]),
    ]
    for copy in copies:
        copy.start()
    for copy in copies:
        copy.wait()
    part = dot(down_ref[...], emb_ref[...], NT)
    for peer in range(parts_ref.shape[0]):
        parts_ref[peer] = part


def second_kernel(parts_ref, key_ref, value_ref, cot_ref, kv_ref, cot_t_ref):
    kv_ref[0] = key_ref[...]
    kv_ref[1] = value_ref[...]
    for head in range(cot_ref.shape[1] // HD):
        at = slice(head * HD, (head + 1) * HD)
        cot_t_ref[at, :] = cot_ref[:, at].astype(F32).T.astype(BF16)


def main_kernel(
    heads_per_step,
    parts_ref,
    up_ref,
    base_ref,
    cot_ref,
    cot_t_ref,
    own_ref,
    near_ref,
    mid_ref,
    far_ref,
    attn_ref,
    inner_parts_ref,
    part_up_ref,
    grad_own_ref,
    grad_near_ref,
    grad_mid_ref,
    grad_far_ref,
    query_ref,
    key_ref,
    value_ref,
    key_t_ref,
    value_t_ref,
    grad_q_ref,
    acc_k_ref,
    acc_v_ref,
):
    rows = base_ref.shape[0]
    heads = base_ref.shape[1] // HD
    inv_scale = 1.0 / math.sqrt(HD)
    to_exp2 = inv_scale * math.log2(math.e)
    n_head = lax.axis_size("head")
    shift = jnp.where(lax.axis_index("head") >= n_head // 2, SPAN // 2, 0)
    rank = lax.rem(lax.axis_index("ctx") + SPAN - shift, SPAN)

    inner = jnp.sum(parts_ref[...], axis=0)
    inner3 = split3(inner)
    for position, ref in enumerate((far_ref, mid_ref, near_ref, own_ref)):
        at = slice(position * rows, (position + 1) * rows)
        key_ref[at, :] = ref[0]
        value_ref[at, :] = ref[1]
        key_t_ref[:, at] = ref[0].astype(F32).T.astype(BF16)
        value_t_ref[:, at] = ref[1].astype(F32).T.astype(BF16)
    acc_k_ref[...] = jnp.zeros_like(acc_k_ref)
    acc_v_ref[...] = jnp.zeros_like(acc_v_ref)

    query_ref[...] = (
        base_ref[...].astype(F32) + 2.0 * dot(inner3, thrice(up_ref[...]), TN)
    ).astype(BF16)
    source = lax.broadcasted_iota(jnp.int32, (rows, rows), 0)
    target = lax.broadcasted_iota(jnp.int32, (rows, rows), 1)
    causal = source <= target
    closed = [jnp.where(rank >= SPAN - 1 - p, 0.0, FAR) for p in range(SPAN - 1)]

    spans = [slice(p * rows, (p + 1) * rows) for p in range(SPAN)]

    def one_head(head):
        at = pl.ds(pl.multiple_of(head * HD, HD), HD)
        query, cot = query_ref[:, at], cot_ref[:, at]
        blocks = [dot(key_ref[span, :], query, NT) for span in spans]
        blocks[-1] = jnp.where(causal, blocks[-1], -FAR)
        tops = [jnp.max(block, axis=0, keepdims=True) for block in blocks]
        top = tops[-1]
        for p in range(SPAN - 1):
            top = jnp.maximum(top, tops[p] - closed[p])
        limits = [top + closed[p] for p in range(SPAN - 1)] + [top]
        powers = [jnp.exp2((b - t) * to_exp2) for b, t in zip(blocks, limits)]
        total = sum(jnp.sum(power, axis=0, keepdims=True) for power in powers)
        inverse = 1.0 / total
        weights = [power * inverse for power in powers]
        weights_b = [weight.astype(BF16) for weight in weights]
        attn_t = sum(dot(value_t_ref[:, span], w) for span, w in zip(spans, weights_b))
        delta = jnp.sum(cot_t_ref[at, :].astype(F32) * attn_t, axis=0, keepdims=True)
        attn_ref[:, at] = attn_t.T.astype(BF16)
        dscores = []
        for span, weight in zip(spans, weights):
            dprob = dot(value_ref[span, :], cot, NT)
            dscores.append((weight * (dprob - delta)).astype(BF16))
        grad_q = sum(dot(key_t_ref[:, span], d) for span, d in zip(spans, dscores))
        grad_q_ref[at, :] = grad_q * (2.0 * inv_scale)
        return query, cot, weights_b, dscores

    def step(i, carry):
        got = [one_head(i * heads_per_step + j) for j in range(heads_per_step)]
        query, cot = (jnp.concatenate([g[k] for g in got], axis=0) for k in (0, 1))
        for p, span in enumerate(spans):
            weight_b, dscore = (
                jnp.concatenate([g[k][p] for g in got], axis=1) for k in (2, 3)
            )
            acc_v_ref[span, :] += dot(weight_b, cot)
            acc_k_ref[span, :] += dot(dscore, query)
        return carry

    lax.fori_loop(0, heads // heads_per_step, step, 0)

    outs = (grad_far_ref, grad_mid_ref, grad_near_ref, grad_own_ref)
    for position, ref in enumerate(outs):
        at = slice(position * rows, (position + 1) * rows)
        ref[0] = (acc_k_ref[at, :] * inv_scale).astype(ref.dtype)
        ref[1] = acc_v_ref[at, :].astype(ref.dtype)

    grad_q = grad_q_ref[...]
    high = grad_q.astype(BF16)
    low = (grad_q - high.astype(F32)).astype(BF16)
    up = up_ref[...]
    grad_inner = dot(up, high) + dot(up, low)
    for peer in range(inner_parts_ref.shape[0]):
        inner_parts_ref[peer] = grad_inner
    r = inner.shape[0]
    rows3 = dot(inner3, high, NT)
    part_up = rows3[:r] + rows3[r : 2 * r] + rows3[2 * r : 3 * r]
    rows3 = dot(inner3, low, NT)
    part_up_ref[...] = part_up + rows3[:r] + rows3[r : 2 * r]


def pieces_kernel(parts_ref, emb_ref, part_up_ref, pieces_ref, terms_ref):
    grad_inner = jnp.sum(parts_ref[...], axis=0)
    r = grad_inner.shape[0]
    terms = split3(grad_inner)
    terms_ref[...] = terms
    rows3 = dot(terms, emb_ref[...])
    part_down = rows3[:r] + rows3[r : 2 * r] + rows3[2 * r : 3 * r]
    half = pieces_ref.shape[0] // 2
    width = pieces_ref.shape[2]
    for piece in range(half):
        at = slice(piece * width, (piece + 1) * width)
        pieces_ref[(piece + TURN) % (2 * half)] = part_down[:, at]
        pieces_ref[(half + piece + TURN) % (2 * half)] = part_up_ref[:, at]


def grad_emb_kernel(terms_ref, down_ref, grad_emb_ref):
    grad_emb_ref[...] = dot(terms_ref[...], thrice(down_ref[...]), TN)


def call(kernel, outs, *args, own=(), scratch=(), limit=SMALL_VMEM, name=None):
    specs = [
        pl.BlockSpec(memory_space=pltpu.HBM if i in own else pltpu.VMEM)
        for i in range(len(args))
    ]
    return pl.pallas_call(
        kernel,
        out_shape=[jax.ShapeDtypeStruct(shape, dtype) for shape, dtype in outs],
        in_specs=specs,
        scratch_shapes=scratch,
        compiler_params=pltpu.CompilerParams(vmem_limit_bytes=limit),
        name=name,
    )(*args)


def ctx_groups(n_ctx, n_head, members):
    return [[c * n_head + h for c in group] for group in members for h in range(n_head)]


def attention(parts, adapter_up, query_base, grad_out, cot_t, kv, near, mid, far):
    rows, width = query_base.shape
    n_head, r, _ = parts.shape
    keys = SPAN * rows
    return call(
        functools.partial(main_kernel, HPS),
        [
            ((rows, width), BF16),
            ((n_head, r, rows), F32),
            ((r, width), F32),
            ((2, rows, HD), F32),
            ((2, rows, HD), BF16),
            ((2, rows, HD), BF16),
            ((2, rows, HD), BF16),
        ],
        parts,
        adapter_up,
        query_base,
        grad_out,
        cot_t,
        kv,
        near,
        mid,
        far,
        scratch=[
            pltpu.VMEM((rows, width), BF16),
            pltpu.VMEM((keys, HD), BF16),
            pltpu.VMEM((keys, HD), BF16),
            pltpu.VMEM((HD, keys), BF16),
            pltpu.VMEM((HD, keys), BF16),
            pltpu.VMEM((width, rows), F32),
            pltpu.VMEM((keys, HD), F32),
            pltpu.VMEM((keys, HD), F32),
        ],
        limit=MAIN_VMEM,
        name="attention",
    )


def heads_of(n_ctx, n_head):
    order = [(h + RH) % n_head for h in range(n_head)]
    return [[c * n_head + h for h in order] for c in range(n_ctx)]


def on_device(embeddings, adapter_down, adapter_up, query_base, key_states, values, grad_out):
    rows, width = query_base.shape
    r = adapter_up.shape[0]
    n_ctx, n_head = lax.axis_size("ctx"), lax.axis_size("head")
    both = ("ctx", "head")
    keys = SPAN * rows
    down_t = adapter_down.T

    def route(distance, back=False):
        pairs = []
        for head in range(n_head):
            shift = SPAN // 2 if head >= n_head // 2 else 0
            for ctx in range(n_ctx):
                if (ctx - shift) % SPAN + distance < SPAN:
                    pair = (ctx * n_head + head, (ctx + distance) % n_ctx * n_head + head)
                    pairs.append(pair[::-1] if back else pair)
        return pairs

    (parts,) = call(
        first_kernel,
        [((n_head, r, rows), F32)],
        embeddings,
        down_t,
        own=(0, 1),
        scratch=[
            pltpu.VMEM(embeddings.shape, BF16),
            pltpu.VMEM(down_t.shape, BF16),
            pltpu.SemaphoreType.DMA((2,)),
        ],
        limit=FIRST_VMEM,
        name="inner_parts",
    )
    kv, cot_t = call(
        second_kernel,
        [((2, rows, HD), BF16), ((width, rows), BF16)],
        parts,
        key_states,
        values,
        grad_out,
        own=(0,),
        name="pack",
    )
    near, mid, far = (lax.ppermute(kv, both, route(d)) for d in (1, 2, 3))
    parts = lax.all_to_all(parts, both, 0, 0, axis_index_groups=heads_of(n_ctx, n_head))
    attn_out, inner_parts, part_up, grad_own, grad_near, grad_mid, grad_far = attention(
        parts, adapter_up, query_base, grad_out, cot_t, kv, near, mid, far
    )
    inner_parts = lax.all_to_all(inner_parts, both, 0, 0, axis_index_groups=heads_of(n_ctx, n_head))

    wide = 16
    blocks = n_ctx // wide
    first_of = [FIRST_LOW if g < blocks // 2 else FIRST_HIGH for g in range(blocks)]
    lists = [
        [g * wide + (m + first_of[g]) % wide for m in range(wide)] for g in range(blocks)
    ]
    block_order = [(g + RM) % blocks for g in range(blocks)]
    every = [[c for g in block_order for c in lists[g]]]
    apart = [[lists[g][m] for g in block_order] for m in range(wide)]
    back = [
        [g * wide + (m + first_of[g] + TURN) % wide for m in range(wide)]
        for g in range(blocks)
    ]
    close, apart, every, back = (
        ctx_groups(n_ctx, n_head, groups) for groups in (lists, apart, every, back)
    )
    piece = 2 * width // wide
    pieces, terms = call(
        pieces_kernel,
        [((wide, r, piece), F32), ((4 * r, rows), BF16)],
        inner_parts,
        embeddings,
        part_up,
        name="adapter_parts",
    )
    (grad_embeddings,) = call(
        grad_emb_kernel,
        [((rows, width), F32)],
        terms,
        down_t,
        name="grad_embeddings",
    )

    def send_terms(after):
        terms = (grad_near, grad_mid, grad_far)
        if after is not None:
            after, *terms = lax.optimization_barrier((after, *terms))
        sent = [
            lax.ppermute(term, both, route(d, back=True))
            for d, term in zip((1, 2, 3), terms)
        ]
        return after, sent

    if TIE == 0:
        _, sent = send_terms(None)
    if TIE == 3:
        _, sent = send_terms(None)
        pieces, *sent = lax.optimization_barrier((pieces, *sent))
    pieces = lax.all_to_all(pieces, both, 0, 0, axis_index_groups=close)
    mine = jnp.sum(pieces, axis=0)
    if TIE == 1:
        mine, sent = send_terms(mine)
    if WIDE_BACK:
        mine = jnp.broadcast_to(mine[None].astype(SENT), (n_ctx, *mine.shape))
        whole = lax.all_to_all(mine, both, 0, 0, axis_index_groups=every)
        whole = jnp.sum(whole.reshape(blocks, wide, r, piece).astype(F32), axis=0)
    else:
        mine = jnp.broadcast_to(mine[None], (blocks, *mine.shape))
        mine = lax.all_to_all(mine, both, 0, 0, axis_index_groups=apart)
        mine = jnp.sum(mine, axis=0)
        mine = jnp.broadcast_to(mine[None], (wide, *mine.shape))
        whole = lax.all_to_all(mine, both, 0, 0, axis_index_groups=back)
    whole = whole.transpose(1, 0, 2).reshape(r, 2 * width)
    grad_adapter_down, grad_adapter_up = whole[:, :width].T, whole[:, width:]

    received = grad_own
    for term in sent:
        received = received + term.astype(F32)
    return (
        attn_out,
        grad_embeddings,
        grad_adapter_down,
        grad_adapter_up,
        received[0],
        received[1],
    )


def solution(mesh):
    in_specs = (
        P("ctx", "head"),
        P("head", None),
        P(None, "head"),
        P("ctx", "head"),
        P("ctx", "head"),
        P("ctx", "head"),
        P("ctx", "head"),
    )
    out_specs = (
        P("ctx", "head"),
        P("ctx", "head"),
        P("head", None),
        P(None, "head"),
        P("ctx", "head"),
        P("ctx", "head"),
    )
    return jax.shard_map(
        on_device, mesh=mesh, in_specs=in_specs, out_specs=out_specs, check_vma=False
    )
```

time: 102 us -> 89.8 us (0.88)
  the two profiles are of different devices: /device:TPU:1 before, /device:TPU:20 now
where the time goes in v2:
time: 89.8 us; the launch traced here: 89.1 us
  starting transfers between devices  36.4 us (41%)
  blocking collectives  24.7 us (28%)
  Pallas kernels  14.2 us (16%)
  waiting for transfers between devices  7.05 us (8%)
  local copies, waits for them, and re-layouts  5.91 us (7%)
    all_to_all x1, blocking collectives, on_device(): lax.all_to_all(parts, both, 0, 0, axis_index_groups=heads_of(n_ctx, n_head))  14.2 us
    pallas_call x5, Pallas kernels, call(): pl.pallas_call(kernel, out_shape=[jax.ShapeDtypeStruct(shape, dtype) for...  14.2 us
    all_to_all x1, starting transfers between devices, on_device(): mine = lax.all_to_all(mine, both, 0, 0, axis_index_groups=apart)  11.2 us
    all_to_all x1, blocking collectives, on_device(): lax.all_to_all(inner_parts, both, 0, 0, axis_index_groups=heads_of(n_ctx,...  10.4 us
    ppermute x3, starting transfers between devices, send_terms(): lax.ppermute(term, both, route(d, back=True))  10.3 us
    all_to_all x1, starting transfers between devices, on_device(): pieces = lax.all_to_all(pieces, both, 0, 0, axis_index_groups=close)  6.75 us
    all_to_all x1, waiting for transfers between devices, on_device(): whole = lax.all_to_all(mine, both, 0, 0, axis_index_groups=back)  4.72 us
    ppermute x3, starting transfers between devices, on_device(): near, mid, far = (lax.ppermute(kv, both, route(d)) for d in (1, 2, 3))  4.33 us
  transfers between devices with their start and end apart: 9, of which 3 were waited for; matrix products, arithmetic and copies ran while one was open for 2% of the time, Pallas kernels for 1%

profile of v2, /device:TPU:20, one launch (start us, length us, event | category | flops | bytes accessed | tf_op | source)
XLA Modules:
  0.0 89.1 jit_solution(14924006829927170332)
XLA Ops:
  0.6 0.0 copy-start
  0.6 1.0 %copy-done = bf16[256,1024]{1,0:T(8,128)(2,1)S(1)} copy-done((bf16[256,1024]{1,0:T(8,128)(2,1)S(1)}, bf16[256,1024]{1,0:T(8,128)(2,1)}, u32[]{:S(2)}) %copy-start) | copy-done | bytes 524312
  1.7 0.7 copy-done.4
  2.4 0.3 inner_parts.1.parts_ref
  2.7 0.7 copy-done.2
  3.4 0.8 copy-done.7
  4.3 0.2 pack.1
  4.5 0.0 copy-start.8
  4.5 0.7 collective-permute-start.2
  5.2 1.3 %collective-permute-start.1 = (bf16[2,256,128]{2,1,0:T(8,128)(2,1)S(1)}, bf16[2,256,128]{2,1,0:T(8,128)(2,1)S(1)}, u32[]{:S(2)}, u32[]{:S(2)}) collective-permute-start(bf16[2,256,128]{2,1,0:T(8,128)(2,1)S(1)} %get-tuple-element.18.own_ref), channel_id=1, source_target_pairs={{0,16},{8,24},{32,48},{40,56},{64,80},{72,88},{96,112},{104,120},{... | collective-permute-start | bytes 393224 | tf_op jit(solution)/shard_map/ppermute | solution.py:310
  6.5 2.4 %collective-permute-start = (bf16[2,256,128]{2,1,0:T(8,128)(2,1)S(1)}, bf16[2,256,128]{2,1,0:T(8,128)(2,1)S(1)}, u32[]{:S(2)}, u32[]{:S(2)}) collective-permute-start(bf16[2,256,128]{2,1,0:T(8,128)(2,1)S(1)} %get-tuple-element.18.own_ref), channel_id=1, source_target_pairs={{0,8},{8,16},{16,24},{32,40},{40,48},{48,56},{64,72},{72,80},{80,8... | collective-permute-start | bytes 393224 | tf_op jit(solution)/shard_map/ppermute | solution.py:310
  8.9 14.2 %all_to_all.25.parts_ref = f32[8,8,256]{2,1,0:T(8,128)S(1)} all-to-all(f32[8,8,256]{2,1,0:T(8,128)S(1)} %inner_parts.1.parts_ref), channel_id=1, replica_groups={{5,6,7,0,1,2,3,4},{13,14,15,8,9,10,11,12},{21,22,23,16,17,18,19,20},{29..., dimensions={0} | all-to-all | bytes 131072 | tf_op jit(solution)/shard_map/all_to_all | solution.py:311
  23.1 0.3 collective-permute-done.1.mid_ref
  23.4 0.0 collective-permute-done.near_ref
  23.4 0.0 copy-start.1
  23.5 11.6 %attention.1 = (bf16[256,1024]{1,0:T(8,128)(2,1)}, f32[8,8,256]{2,1,0:T(8,128)S(1)}, f32[8,1024]{1,0:T(8,128)S(1)}, f32[2,256,128]{2,1,0:T(8,128)S(1)}, bf16[2,2...) custom-call(f32[8,8,256]{2,1,0:T(8,128)S(1)} %all_to_all.25.parts_ref, ...), custom_call_target="tpu_custom_call" | custom-call | tf_op jit(solution)/shard_map/attention/pallas_call | solution.py:210
  35.0 10.4 %all_to_all.26.parts_ref = f32[8,8,256]{2,1,0:T(8,128)S(1)} all-to-all(f32[8,8,256]{2,1,0:T(8,128)S(1)} %get-tuple-element.20), channel_id=1, replica_groups={{5,6,7,0,1,2,3,4},{13,14,15,8,9,10,11,12},{21,22,23,16,17,18,19,20},{29..., dimensions={0} | all-to-all | bytes 131072 | tf_op jit(solution)/shard_map/all_to_all | solution.py:315
  45.5 0.8 adapter_parts.1
  46.3 6.7 %all-to-all-start.2 = ((f32[16,8,128]{2,1,0:T(8,128)}), f32[16,8,128]{2,1,0:T(8,128)S(1)}, u32[]{:S(2)}, u32[]{:S(2)}) async-start(f32[16,8,128]{2,1,0:T(8,128)} %get-tuple-element.23), calls=%async_computation.2 | async-start | bytes 131072 | tf_op jit(solution)/shard_map/all_to_all | solution.py:365
  53.0 8.1 %collective-permute-start.3 = (bf16[2,256,128]{2,1,0:T(8,128)(2,1)S(1)}, bf16[2,256,128]{2,1,0:T(8,128)(2,1)S(1)}, u32[]{:S(2)}, u32[]{:S(2)}) collective-permute-start(bf16[2,256,128]{2,1,0:T(8,128)(2,1)S(1)} %get-tuple-element.25), channel_id=1, source_target_pairs={{8,0},{16,8},{24,16},{40,32},{48,40},{56,48},{72,64},{80,72},{88,8... | collective-permute-start | bytes 393224 | tf_op jit(solution)/shard_map/ppermute | solution.py:355
  61.2 1.5 %collective-permute-start.4 = (bf16[2,256,128]{2,1,0:T(8,128)(2,1)S(1)}, bf16[2,256,128]{2,1,0:T(8,128)(2,1)S(1)}, u32[]{:S(2)}, u32[]{:S(2)}) collective-permute-start(bf16[2,256,128]{2,1,0:T(8,128)(2,1)S(1)} %get-tuple-element.26), channel_id=1, source_target_pairs={{16,0},{24,8},{48,32},{56,40},{80,64},{88,72},{112,96},{120,104},{... | collective-permute-start | bytes 393224 | tf_op jit(solution)/shard_map/ppermute | solution.py:355
  62.7 0.7 collective-permute-start.5
  63.4 0.6 broadcast_in_dim.4
  64.0 11.2 %all-to-all-start.3 = ((f32[4,8,128]{2,1,0:T(8,128)}), f32[4,8,128]{2,1,0:T(8,128)S(1)}, u32[]{:S(2)}, u32[]{:S(2)}) async-start(f32[4,8,128]{2,1,0:T(8,128)} %broadcast_in_dim.4), calls=%async_computation.3 | async-start | bytes 32768 | tf_op jit(solution)/shard_map/all_to_all | solution.py:375
  75.3 1.3 %grad_embeddings.1 = f32[256,1024]{1,0:T(8,128)} custom-call(bf16[32,256]{1,0:T(8,128)(2,1)S(1)} %get-tuple-element.22.terms_ref, bf16[8,1024]{1,0:T(8,128)(2,1)S(1)} %bitcast.11), custom_call_target="tpu_custom_call" | custom-call | tf_op jit(solution)/shard_map/grad_embeddings/pallas_call | solution.py:210
  76.6 2.0 %all-to-all-done.3 = f32[4,8,128]{2,1,0:T(8,128)S(1)} async-done(((f32[4,8,128]{2,1,0:T(8,128)}), f32[4,8,128]{2,1,0:T(8,128)S(1)}, u32[]{:S(2)}, u32[]{:S(2)}) %all-to-all-start.3) | async-done | bytes 16416 | tf_op jit(solution)/shard_map/all_to_all | solution.py:375
  78.5 0.6 broadcast_in_dim.5
  79.1 3.8 %all-to-all-start.4 = ((f32[16,8,128]{2,1,0:T(8,128)}), f32[16,8,128]{2,1,0:T(8,128)S(1)}, u32[]{:S(2)}, u32[]{:S(2)}) async-start(f32[16,8,128]{2,1,0:T(8,128)} %broadcast_in_dim.5), calls=%async_computation.4 | async-start | bytes 131072 | tf_op jit(solution)/shard_map/all_to_all | solution.py:378
  82.9 0.1 convert_add_fusion
  83.0 0.7 slice_bitcast_fusion
  83.7 4.7 %all-to-all-done.4 = f32[16,8,128]{2,1,0:T(8,128)S(1)} async-done(((f32[16,8,128]{2,1,0:T(8,128)}), f32[16,8,128]{2,1,0:T(8,128)S(1)}, u32[]{:S(2)}, u32[]{:S(2)}) %all-to-all-start.4) | async-done | bytes 65568 | tf_op jit(solution)/shard_map/all_to_all | solution.py:378
  88.4 0.6 fusion
  (18 shorter events, 0.1 us)
Async XLA Ops:
  0.6 1.0 %copy-start = (bf16[256,1024]{1,0:T(8,128)(2,1)S(1)}, bf16[256,1024]{1,0:T(8,128)(2,1)}, u32[]{:S(2)}) copy-start(bf16[256,1024]{1,0:T(8,128)(2,1)} %emb_ref.1) | copy-start | bytes 1572868
  1.7 0.7 copy-start.4
  2.4 1.0 %copy-start.2 = (bf16[256,1024]{1,0:T(8,128)(2,1)S(1)}, bf16[256,1024]{1,0:T(8,128)(2,1)}, u32[]{:S(2)}) copy-start(bf16[256,1024]{1,0:T(8,128)(2,1)} %cot_ref.3) | copy-start | bytes 1572868
  2.4 1.0 %copy-start.6 = (bf16[256,128]{1,0:T(8,128)(2,1)S(1)}, bf16[256,128]{1,0:T(8,128)(2,1)}, u32[]{:S(2)}) copy-start(bf16[256,128]{1,0:T(8,128)(2,1)} %key_ref.1) | copy-start | bytes 196612
  3.4 0.8 copy-start.7
  4.3 19.2 %copy-start.3 = (bf16[256,1024]{1,0:T(8,128)(2,1)S(1)}, bf16[256,1024]{1,0:T(8,128)(2,1)}, u32[]{:S(2)}) copy-start(bf16[256,1024]{1,0:T(8,128)(2,1)} %base_ref.1) | copy-start | bytes 1572868
  4.5 19.0 %copy-start.8 = (bf16[8,1024]{1,0:T(8,128)(2,1)S(1)}, bf16[8,1024]{1,0:T(8,128)(2,1)}, u32[]{:S(2)}) copy-start(bf16[8,1024]{1,0:T(8,128)(2,1)} %up_ref.1) | copy-start | bytes 49156
  4.5 18.6 %collective-permute-start.2 = (bf16[2,256,128]{2,1,0:T(8,128)(2,1)S(1)}, bf16[2,256,128]{2,1,0:T(8,128)(2,1)S(1)}, u32[]{:S(2)}, u32[]{:S(2)}) collective-permute-start(bf16[2,256,128]{2,1,0:T(8,128)(2,1)S(1)} %get-tuple-element.18.own_ref), channel_id=1, source_target_pairs={{0,24},{32,56},{64,88},{96,120},{128,152},{160,184},{192,216},{224... | collective-permute-start | bytes 393224 | tf_op jit(solution)/shard_map/ppermute | solution.py:310
  5.2 18.3 %collective-permute-start.1 = (bf16[2,256,128]{2,1,0:T(8,128)(2,1)S(1)}, bf16[2,256,128]{2,1,0:T(8,128)(2,1)S(1)}, u32[]{:S(2)}, u32[]{:S(2)}) collective-permute-start(bf16[2,256,128]{2,1,0:T(8,128)(2,1)S(1)} %get-tuple-element.18.own_ref), channel_id=1, source_target_pairs={{0,16},{8,24},{32,48},{40,56},{64,80},{72,88},{96,112},{104,120},{... | collective-permute-start | bytes 393224 | tf_op jit(solution)/shard_map/ppermute | solution.py:310
  6.5 17.0 %collective-permute-start = (bf16[2,256,128]{2,1,0:T(8,128)(2,1)S(1)}, bf16[2,256,128]{2,1,0:T(8,128)(2,1)S(1)}, u32[]{:S(2)}, u32[]{:S(2)}) collective-permute-start(bf16[2,256,128]{2,1,0:T(8,128)(2,1)S(1)} %get-tuple-element.18.own_ref), channel_id=1, source_target_pairs={{0,8},{8,16},{16,24},{32,40},{40,48},{48,56},{64,72},{72,80},{80,8... | collective-permute-start | bytes 393224 | tf_op jit(solution)/shard_map/ppermute | solution.py:310
  23.4 22.0 %copy-start.1 = (bf16[256,1024]{1,0:T(8,128)(2,1)S(1)}, bf16[256,1024]{1,0:T(8,128)(2,1)}, u32[]{:S(2)}) copy-start(bf16[256,1024]{1,0:T(8,128)(2,1)} %emb_ref.1) | copy-start | bytes 1572868
  46.3 17.1 %all-to-all-start.2 = ((f32[16,8,128]{2,1,0:T(8,128)}), f32[16,8,128]{2,1,0:T(8,128)S(1)}, u32[]{:S(2)}, u32[]{:S(2)}) async-start(f32[16,8,128]{2,1,0:T(8,128)} %get-tuple-element.23), calls=%async_computation.2 | async-start | bytes 131072 | tf_op jit(solution)/shard_map/all_to_all | solution.py:365
  53.0 29.9 %collective-permute-start.3 = (bf16[2,256,128]{2,1,0:T(8,128)(2,1)S(1)}, bf16[2,256,128]{2,1,0:T(8,128)(2,1)S(1)}, u32[]{:S(2)}, u32[]{:S(2)}) collective-permute-start(bf16[2,256,128]{2,1,0:T(8,128)(2,1)S(1)} %get-tuple-element.25), channel_id=1, source_target_pairs={{8,0},{16,8},{24,16},{40,32},{48,40},{56,48},{72,64},{80,72},{88,8... | collective-permute-start | bytes 393224 | tf_op jit(solution)/shard_map/ppermute | solution.py:355
  61.2 21.8 %collective-permute-start.4 = (bf16[2,256,128]{2,1,0:T(8,128)(2,1)S(1)}, bf16[2,256,128]{2,1,0:T(8,128)(2,1)S(1)}, u32[]{:S(2)}, u32[]{:S(2)}) collective-permute-start(bf16[2,256,128]{2,1,0:T(8,128)(2,1)S(1)} %get-tuple-element.26), channel_id=1, source_target_pairs={{16,0},{24,8},{48,32},{56,40},{80,64},{88,72},{112,96},{120,104},{... | collective-permute-start | bytes 393224 | tf_op jit(solution)/shard_map/ppermute | solution.py:355
  62.7 20.2 %collective-permute-start.5 = (bf16[2,256,128]{2,1,0:T(8,128)(2,1)S(1)}, bf16[2,256,128]{2,1,0:T(8,128)(2,1)S(1)}, u32[]{:S(2)}, u32[]{:S(2)}) collective-permute-start(bf16[2,256,128]{2,1,0:T(8,128)(2,1)S(1)} %get-tuple-element.27), channel_id=1, source_target_pairs={{24,0},{56,32},{88,64},{120,96},{152,128},{184,160},{216,192},{248... | collective-permute-start | bytes 393224 | tf_op jit(solution)/shard_map/ppermute | solution.py:355
  64.0 11.2 %copy-start.5 = (bf16[1024,8]{0,1:T(8,128)(2,1)S(1)}, bf16[1024,8]{0,1:T(8,128)(2,1)}, u32[]{:S(2)}) copy-start(bf16[1024,8]{0,1:T(8,128)(2,1)} %param.8) | copy-start | bytes 49156
  64.0 14.5 %all-to-all-start.3 = ((f32[4,8,128]{2,1,0:T(8,128)}), f32[4,8,128]{2,1,0:T(8,128)S(1)}, u32[]{:S(2)}, u32[]{:S(2)}) async-start(f32[4,8,128]{2,1,0:T(8,128)} %broadcast_in_dim.4), calls=%async_computation.3 | async-start | bytes 32768 | tf_op jit(solution)/shard_map/all_to_all | solution.py:375
  79.1 9.3 %all-to-all-start.4 = ((f32[16,8,128]{2,1,0:T(8,128)}), f32[16,8,128]{2,1,0:T(8,128)S(1)}, u32[]{:S(2)}, u32[]{:S(2)}) async-start(f32[16,8,128]{2,1,0:T(8,128)} %broadcast_in_dim.5), calls=%async_computation.4 | async-start | bytes 131072 | tf_op jit(solution)/shard_map/all_to_all | solution.py:378

commit v3 on v2

--- a/solution.py
+++ b/solution.py
@@ -14,11 +14,14 @@
 RM = 2
 RH = 5
 FIRST_LOW = 12
-FIRST_HIGH = 0
-TURN = 8
-WIDE_BACK = False
-SENT = jnp.float32
-FIRST_VMEM = 16 * 2**20
+FIRST_HIGH = 8
+TURN = 0
+WIDE_BACK = True
+SENT = jnp.bfloat16
+FIRST_VMEM = 60 * 2**20
+TURN_COST = 0
+Q_COST = 0
+EMB_COST = 0
 SPAN = 4
 FAR = 1e30
 F32 = jnp.float32
@@ -46,26 +49,59 @@
     return jnp.concatenate([x, x, x, jnp.zeros_like(x)], axis=0).astype(BF16)
 
 
-def first_kernel(emb_hbm, down_hbm, parts_ref, emb_ref, down_ref, sems):
-    copies = [
-        pltpu.make_async_copy(down_hbm, down_ref, sems.at[0]),
-        pltpu.make_async_copy(emb_hbm, emb_ref, sems.at[1]),
-    ]
+def first_kernel(
+    emb_hbm, down_hbm, key_hbm, value_hbm, parts_ref, kv_ref, emb_ref, down_ref, sems
+):
+    pairs = (
+        (down_hbm, down_ref),
+        (emb_hbm, emb_ref),
+        (key_hbm, kv_ref.at[0]),
+        (value_hbm, kv_ref.at[1]),
+    )
+    copies = [pltpu.make_async_copy(a, b, sems.at[i]) for i, (a, b) in enumerate(pairs)]
     for copy in copies:
         copy.start()
-    for copy in copies:
-        copy.wait()
+    copies[0].wait()
+    copies[1].wait()
     part = dot(down_ref[...], emb_ref[...], NT)
     for peer in range(parts_ref.shape[0]):
         parts_ref[peer] = part
-
-
-def second_kernel(parts_ref, key_ref, value_ref, cot_ref, kv_ref, cot_t_ref):
-    kv_ref[0] = key_ref[...]
-    kv_ref[1] = value_ref[...]
+    copies[2].wait()
+    copies[3].wait()
+
+
+def final_kernel(whole_ref, own_ref, near_ref, mid_ref, far_ref, *outs):
+    down_ref, up_ref, grad_key_ref, grad_value_ref = outs
+    pieces, _, width = whole_ref.shape
+    half = pieces // 2
+    for piece in range(half):
+        at = slice(piece * width, (piece + 1) * width)
+        down_ref[:, at] = whole_ref[piece]
+        up_ref[:, at] = whole_ref[half + piece]
+    for i, ref in enumerate((grad_key_ref, grad_value_ref)):
+        terms = [term[i].astype(F32) for term in (near_ref, mid_ref, far_ref)]
+        ref[...] = own_ref[i] + terms[0] + terms[1] + terms[2]
+
+
+def turn_kernel(
+    own_ref, near_ref, mid_ref, far_ref, cot_ref, key_ref, value_ref, key_t_ref, value_t_ref, cot_t_ref
+):
+    rows = own_ref.shape[1]
+    for position, ref in enumerate((far_ref, mid_ref, near_ref, own_ref)):
+        at = slice(position * rows, (position + 1) * rows)
+        key_ref[at, :] = ref[0]
+        value_ref[at, :] = ref[1]
+        key_t_ref[:, at] = ref[0].astype(F32).T.astype(BF16)
+        value_t_ref[:, at] = ref[1].astype(F32).T.astype(BF16)
     for head in range(cot_ref.shape[1] // HD):
         at = slice(head * HD, (head + 1) * HD)
         cot_t_ref[at, :] = cot_ref[:, at].astype(F32).T.astype(BF16)
+
+
+def spread_kernel(terms_ref, out_ref):
+    total = jnp.sum(terms_ref[...], axis=0)
+    for peer in range(out_ref.shape[0]):
+        out_ref[peer] = total.astype(out_ref.dtype)
 
 
 def main_kernel(
@@ -75,10 +111,10 @@
     base_ref,
     cot_ref,
     cot_t_ref,
-    own_ref,
-    near_ref,
-    mid_ref,
-    far_ref,
+    key_ref,
+    value_ref,
+    key_t_ref,
+    value_t_ref,
     attn_ref,
     inner_parts_ref,
     part_up_ref,
@@ -87,10 +123,6 @@
     grad_mid_ref,
     grad_far_ref,
     query_ref,
-    key_ref,
-    value_ref,
-    key_t_ref,
-    value_t_ref,
     grad_q_ref,
     acc_k_ref,
     acc_v_ref,
@@ -103,20 +135,13 @@
     shift = jnp.where(lax.axis_index("head") >= n_head // 2, SPAN // 2, 0)
     rank = lax.rem(lax.axis_index("ctx") + SPAN - shift, SPAN)
 
-    inner = jnp.sum(parts_ref[...], axis=0)
-    inner3 = split3(inner)
-    for position, ref in enumerate((far_ref, mid_ref, near_ref, own_ref)):
-        at = slice(position * rows, (position + 1) * rows)
-        key_ref[at, :] = ref[0]
-        value_ref[at, :] = ref[1]
-        key_t_ref[:, at] = ref[0].astype(F32).T.astype(BF16)
-        value_t_ref[:, at] = ref[1].astype(F32).T.astype(BF16)
-    acc_k_ref[...] = jnp.zeros_like(acc_k_ref)
-    acc_v_ref[...] = jnp.zeros_like(acc_v_ref)
-
+    inner3 = split3(jnp.sum(parts_ref[...], axis=0))
     query_ref[...] = (
         base_ref[...].astype(F32) + 2.0 * dot(inner3, thrice(up_ref[...]), TN)
     ).astype(BF16)
+    acc_k_ref[...] = jnp.zeros_like(acc_k_ref)
+    acc_v_ref[...] = jnp.zeros_like(acc_v_ref)
+
     source = lax.broadcasted_iota(jnp.int32, (rows, rows), 0)
     target = lax.broadcasted_iota(jnp.int32, (rows, rows), 1)
     causal = source <= target
@@ -176,7 +201,7 @@
     grad_inner = dot(up, high) + dot(up, low)
     for peer in range(inner_parts_ref.shape[0]):
         inner_parts_ref[peer] = grad_inner
-    r = inner.shape[0]
+    r = up.shape[0]
     rows3 = dot(inner3, high, NT)
     part_up = rows3[:r] + rows3[r : 2 * r] + rows3[2 * r : 3 * r]
     rows3 = dot(inner3, low, NT)
@@ -202,7 +227,9 @@
     grad_emb_ref[...] = dot(terms_ref[...], thrice(down_ref[...]), TN)
 
 
-def call(kernel, outs, *args, own=(), scratch=(), limit=SMALL_VMEM, name=None):
+def call(
+    kernel, outs, *args, own=(), own_out=(), scratch=(), limit=SMALL_VMEM, cost=0, name=None
+):
     specs = [
         pl.BlockSpec(memory_space=pltpu.HBM if i in own else pltpu.VMEM)
         for i in range(len(args))
@@ -211,6 +238,13 @@
         kernel,
         out_shape=[jax.ShapeDtypeStruct(shape, dtype) for shape, dtype in outs],
         in_specs=specs,
+        out_specs=[
+            pl.BlockSpec(memory_space=pltpu.HBM if i in own_out else pltpu.VMEM)
+            for i in range(len(outs))
+        ],
+        cost_estimate=pl.CostEstimate(flops=0, bytes_accessed=cost, transcendentals=0)
+        if cost
+        else None,
         scratch_shapes=scratch,
         compiler_params=pltpu.CompilerParams(vmem_limit_bytes=limit),
         name=name,
@@ -221,7 +255,7 @@
     return [[c * n_head + h for c in group] for group in members for h in range(n_head)]
 
 
-def attention(parts, adapter_up, query_base, grad_out, cot_t, kv, near, mid, far):
+def attention(parts, adapter_up, query_base, grad_out, turned):
     rows, width = query_base.shape
     n_head, r, _ = parts.shape
     keys = SPAN * rows
@@ -240,17 +274,9 @@
         adapter_up,
         query_base,
         grad_out,
-        cot_t,
-        kv,
-        near,
-        mid,
-        far,
+        *turned,
         scratch=[
             pltpu.VMEM((rows, width), BF16),
-            pltpu.VMEM((keys, HD), BF16),
-            pltpu.VMEM((keys, HD), BF16),
-            pltpu.VMEM((HD, keys), BF16),
-            pltpu.VMEM((HD, keys), BF16),
             pltpu.VMEM((width, rows), F32),
             pltpu.VMEM((keys, HD), F32),
             pltpu.VMEM((keys, HD), F32),
@@ -258,6 +284,13 @@
         limit=MAIN_VMEM,
         name="attention",
     )
+
+
+def spread(terms, peers, dtype):
+    (out,) = call(
+        spread_kernel, [((peers, *terms.shape[1:]), dtype)], terms, name="spread"
+    )
+    return out
 
 
 def heads_of(n_ctx, n_head):
@@ -283,34 +316,42 @@
                     pairs.append(pair[::-1] if back else pair)
         return pairs
 
-    (parts,) = call(
+    parts, kv = call(
         first_kernel,
-        [((n_head, r, rows), F32)],
+        [((n_head, r, rows), F32), ((2, rows, HD), BF16)],
         embeddings,
         down_t,
-        own=(0, 1),
+        key_states,
+        values,
+        own=(0, 1, 2, 3),
         scratch=[
             pltpu.VMEM(embeddings.shape, BF16),
             pltpu.VMEM(down_t.shape, BF16),
-            pltpu.SemaphoreType.DMA((2,)),
+            pltpu.SemaphoreType.DMA((4,)),
         ],
         limit=FIRST_VMEM,
         name="inner_parts",
     )
-    kv, cot_t = call(
-        second_kernel,
-        [((2, rows, HD), BF16), ((width, rows), BF16)],
-        parts,
-        key_states,
-        values,
-        grad_out,
-        own=(0,),
-        name="pack",
-    )
     near, mid, far = (lax.ppermute(kv, both, route(d)) for d in (1, 2, 3))
     parts = lax.all_to_all(parts, both, 0, 0, axis_index_groups=heads_of(n_ctx, n_head))
+    key, value, key_t, value_t, cot_t = call(
+        turn_kernel,
+        [
+            ((keys, HD), BF16),
+            ((keys, HD), BF16),
+            ((HD, keys), BF16),
+            ((HD, keys), BF16),
+            ((width, rows), BF16),
+        ],
+        kv,
+        near,
+        mid,
+        far,
+        grad_out,
+        name="turn",
+    )
     attn_out, inner_parts, part_up, grad_own, grad_near, grad_mid, grad_far = attention(
-        parts, adapter_up, query_base, grad_out, cot_t, kv, near, mid, far
+        parts, adapter_up, query_base, grad_out, (cot_t, key, value, key_t, value_t)
     )
     inner_parts = lax.all_to_all(inner_parts, both, 0, 0, axis_index_groups=heads_of(n_ctx, n_head))
 
@@ -344,6 +385,7 @@
         [((rows, width), F32)],
         terms,
         down_t,
+        cost=EMB_COST,
         name="grad_embeddings",
     )
 
@@ -363,33 +405,27 @@
         _, sent = send_terms(None)
         pieces, *sent = lax.optimization_barrier((pieces, *sent))
     pieces = lax.all_to_all(pieces, both, 0, 0, axis_index_groups=close)
-    mine = jnp.sum(pieces, axis=0)
+    mine = pieces
     if TIE == 1:
         mine, sent = send_terms(mine)
     if WIDE_BACK:
-        mine = jnp.broadcast_to(mine[None].astype(SENT), (n_ctx, *mine.shape))
+        mine = spread(mine, n_ctx, SENT)
         whole = lax.all_to_all(mine, both, 0, 0, axis_index_groups=every)
         whole = jnp.sum(whole.reshape(blocks, wide, r, piece).astype(F32), axis=0)
     else:
-        mine = jnp.broadcast_to(mine[None], (blocks, *mine.shape))
+        mine = spread(mine, blocks, F32)
         mine = lax.all_to_all(mine, both, 0, 0, axis_index_groups=apart)
-        mine = jnp.sum(mine, axis=0)
-        mine = jnp.broadcast_to(mine[None], (wide, *mine.shape))
+        mine = spread(mine, wide, F32)
         whole = lax.all_to_all(mine, both, 0, 0, axis_index_groups=back)
-    whole = whole.transpose(1, 0, 2).reshape(r, 2 * width)
-    grad_adapter_down, grad_adapter_up = whole[:, :width].T, whole[:, width:]
-
-    received = grad_own
-    for term in sent:
-        received = received + term.astype(F32)
-    return (
-        attn_out,
-        grad_embeddings,
-        grad_adapter_down,
-        grad_adapter_up,
-        received[0],
-        received[1],
-    )
+    grad_down, grad_up, grad_key, grad_value = call(
+        final_kernel,
+        [((r, width), F32), ((r, width), F32), ((rows, HD), F32), ((rows, HD), F32)],
+        whole,
+        grad_own,
+        *sent,
+        name="final",
+    )
+    return (attn_out, grad_embeddings, grad_down.T, grad_up, grad_key, grad_value)
 
 
 def solution(mesh):

time: 89.8 us -> 85.5 us (0.952)
  the two profiles are of different devices: /device:TPU:20 before, /device:TPU:28 now
where the time goes in v3:
time: 85.5 us; the launch traced here: 85 us
  starting transfers between devices  29.5 us (35%)
  blocking collectives  20.4 us (24%)
  waiting for transfers between devices  17.5 us (20%)
  Pallas kernels  16.8 us (20%)
    pallas_call x7, Pallas kernels, call(): pl.pallas_call(kernel, out_shape=[jax.ShapeDtypeStruct(shape, dtype) for...  16.8 us
    all_to_all x1, starting transfers between devices, on_device(): whole = lax.all_to_all(mine, both, 0, 0, axis_index_groups=every)  15.4 us
    all_to_all x1, blocking collectives, on_device(): lax.all_to_all(inner_parts, both, 0, 0, axis_index_groups=heads_of(n_ctx,...  11.8 us
    all_to_all x1, waiting for transfers between devices, on_device(): lax.all_to_all(parts, both, 0, 0, axis_index_groups=heads_of(n_ctx, n_head))  8.75 us
    all_to_all x1, blocking collectives, on_device(): pieces = lax.all_to_all(pieces, both, 0, 0, axis_index_groups=close)  8.59 us
    ppermute x3, starting transfers between devices, on_device(): near, mid, far = (lax.ppermute(kv, both, route(d)) for d in (1, 2, 3))  6.9 us
    ppermute x3, waiting for transfers between devices, send_terms(): lax.ppermute(term, both, route(d, back=True))  5.02 us
    ppermute x3, starting transfers between devices, send_terms(): lax.ppermute(term, both, route(d, back=True))  3.88 us
  transfers between devices with their start and end apart: 8, of which 4 were waited for; matrix products, arithmetic and copies ran while one was open for 0% of the time, Pallas kernels for 2%

profile of v3, /device:TPU:28, one launch (start us, length us, event | category | flops | bytes accessed | tf_op | source)
XLA Modules:
  0.0 85.0 jit_solution(13766932225714647612)
XLA Ops:
  0.6 0.0 copy-start.1
  0.6 2.1 %inner_parts.1 = (f32[8,8,256]{2,1,0:T(8,128)}, bf16[2,256,128]{2,1,0:T(8,128)(2,1)}) custom-call(bf16[256,1024]{1,0:T(8,128)(2,1)} %emb_ref.1, bf16[8,1024]{1,0:T(8,128)(2,1)} %bitcast.4, bf16[256,128]{1,0:T(8,128)(2,1)} %key_hbm.1, bf16[256,128]{1,0:T(8,128)(2,1)} %value_hbm.1), custom_call_target="tpu_custom_call" | custom-call | tf_op jit(solution)/shard_map/inner_parts/pallas_call | solution.py:237
  2.7 0.0 copy-start.3
  2.7 3.6 %collective-permute-start.2 = (bf16[2,256,128]{2,1,0:T(8,128)(2,1)}, bf16[2,256,128]{2,1,0:T(8,128)(2,1)S(1)}, u32[]{:S(2)}, u32[]{:S(2)}) collective-permute-start(bf16[2,256,128]{2,1,0:T(8,128)(2,1)} %get-tuple-element.27.own_ref), channel_id=1, source_target_pairs={{0,24},{32,56},{64,88},{96,120},{128,152},{160,184},{192,216},{224... | collective-permute-start | bytes 393224 | tf_op jit(solution)/shard_map/ppermute | solution.py:335
  6.3 1.3 %collective-permute-start.1 = (bf16[2,256,128]{2,1,0:T(8,128)(2,1)}, bf16[2,256,128]{2,1,0:T(8,128)(2,1)S(1)}, u32[]{:S(2)}, u32[]{:S(2)}) collective-permute-start(bf16[2,256,128]{2,1,0:T(8,128)(2,1)} %get-tuple-element.27.own_ref), channel_id=1, source_target_pairs={{0,16},{8,24},{32,48},{40,56},{64,80},{72,88},{96,112},{104,120},{... | collective-permute-start | bytes 393224 | tf_op jit(solution)/shard_map/ppermute | solution.py:335
  7.6 2.0 %collective-permute-start = (bf16[2,256,128]{2,1,0:T(8,128)(2,1)}, bf16[2,256,128]{2,1,0:T(8,128)(2,1)S(1)}, u32[]{:S(2)}, u32[]{:S(2)}) collective-permute-start(bf16[2,256,128]{2,1,0:T(8,128)(2,1)} %get-tuple-element.27.own_ref), channel_id=1, source_target_pairs={{0,8},{8,16},{16,24},{32,40},{40,48},{48,56},{64,72},{72,80},{80,8... | collective-permute-start | bytes 393224 | tf_op jit(solution)/shard_map/ppermute | solution.py:335
  9.7 3.4 %all-to-all-start = ((f32[8,8,256]{2,1,0:T(8,128)}), f32[8,8,256]{2,1,0:T(8,128)S(1)}, u32[]{:S(2)}, u32[]{:S(2)}) async-start(f32[8,8,256]{2,1,0:T(8,128)} %get-tuple-element.26), calls=%async_computation | async-start | bytes 131072 | tf_op jit(solution)/shard_map/all_to_all | solution.py:336
  13.0 0.0 copy-start.2
  13.1 0.0 collective-permute-done.2.far_ref
  13.1 0.0 collective-permute-done.1.mid_ref
  13.1 0.0 collective-permute-done.near_ref
  13.1 0.0 copy-done.1
  13.1 0.0 copy-done.3
  13.1 0.0 copy-start.5
  13.1 0.3 turn.1
  13.5 8.7 %all-to-all-done.parts_ref = f32[8,8,256]{2,1,0:T(8,128)S(1)} async-done(((f32[8,8,256]{2,1,0:T(8,128)}), f32[8,8,256]{2,1,0:T(8,128)S(1)}, u32[]{:S(2)}, u32[]{:S(2)}) %all-to-all-start) | async-done | bytes 65568 | tf_op jit(solution)/shard_map/all_to_all | solution.py:336
  22.2 0.0 copy-done.2
  22.2 11.5 %attention.1 = (bf16[256,1024]{1,0:T(8,128)(2,1)}, f32[8,8,256]{2,1,0:T(8,128)S(1)}, f32[8,1024]{1,0:T(8,128)S(1)}, f32[2,256,128]{2,1,0:T(8,128)S(1)}, bf16[2,2...) custom-call(f32[8,8,256]{2,1,0:T(8,128)S(1)} %all-to-all-done.parts_ref, ...), custom_call_target="tpu_custom_call" | custom-call | tf_op jit(solution)/shard_map/attention/pallas_call | solution.py:237
  33.7 11.8 %all_to_all.20.parts_ref = f32[8,8,256]{2,1,0:T(8,128)S(1)} all-to-all(f32[8,8,256]{2,1,0:T(8,128)S(1)} %get-tuple-element.34), channel_id=1, replica_groups={{5,6,7,0,1,2,3,4},{13,14,15,8,9,10,11,12},{21,22,23,16,17,18,19,20},{29..., dimensions={0} | all-to-all | bytes 131072 | tf_op jit(solution)/shard_map/all_to_all | solution.py:356
  45.5 0.2 adapter_parts.1
  45.6 8.6 %all_to_all.21.terms_ref = f32[16,8,128]{2,1,0:T(8,128)S(1)} all-to-all(f32[16,8,128]{2,1,0:T(8,128)S(1)} %get-tuple-element.37), channel_id=1, replica_groups={{96,104,112,120,0,8,16,24,32,40,48,56,64,72,80,88},{97,105,113,121,1,9,..., dimensions={0} | all-to-all | bytes 131072 | tf_op jit(solution)/shard_map/all_to_all | solution.py:407
  54.2 0.7 spread.1
  54.9 15.4 %all-to-all-start.3 = ((bf16[64,8,128]{2,1,0:T(8,128)(2,1)}), bf16[64,8,128]{2,1,0:T(8,128)(2,1)S(1)}, u32[]{:S(2)}, u32[]{:S(2)}) async-start(bf16[64,8,128]{2,1,0:T(8,128)(2,1)} %spread.1), calls=%async_computation.3 | async-start | bytes 262144 | tf_op jit(solution)/shard_map/all_to_all | solution.py:413
  70.3 1.3 %collective-permute-start.3 = (bf16[2,256,128]{2,1,0:T(8,128)(2,1)S(1)}, bf16[2,256,128]{2,1,0:T(8,128)(2,1)S(1)}, u32[]{:S(2)}, u32[]{:S(2)}) collective-permute-start(bf16[2,256,128]{2,1,0:T(8,128)(2,1)S(1)} %get-tuple-element.39), channel_id=1, source_target_pairs={{8,0},{16,8},{24,16},{40,32},{48,40},{56,48},{72,64},{80,72},{88,8... | collective-permute-start | bytes 393224 | tf_op jit(solution)/shard_map/ppermute | solution.py:397
  71.6 1.3 %collective-permute-start.4 = (bf16[2,256,128]{2,1,0:T(8,128)(2,1)S(1)}, bf16[2,256,128]{2,1,0:T(8,128)(2,1)S(1)}, u32[]{:S(2)}, u32[]{:S(2)}) collective-permute-start(bf16[2,256,128]{2,1,0:T(8,128)(2,1)S(1)} %get-tuple-element.40), channel_id=1, source_target_pairs={{16,0},{24,8},{48,32},{56,40},{80,64},{88,72},{112,96},{120,104},{... | collective-permute-start | bytes 393224 | tf_op jit(solution)/shard_map/ppermute | solution.py:397
  72.9 1.3 %collective-permute-start.5 = (bf16[2,256,128]{2,1,0:T(8,128)(2,1)S(1)}, bf16[2,256,128]{2,1,0:T(8,128)(2,1)S(1)}, u32[]{:S(2)}, u32[]{:S(2)}) collective-permute-start(bf16[2,256,128]{2,1,0:T(8,128)(2,1)S(1)} %get-tuple-element.41), channel_id=1, source_target_pairs={{24,0},{56,32},{88,64},{120,96},{152,128},{184,160},{216,192},{248... | collective-permute-start | bytes 393224 | tf_op jit(solution)/shard_map/ppermute | solution.py:397
  74.2 1.3 %grad_embeddings.1 = f32[256,1024]{1,0:T(8,128)} custom-call(bf16[32,256]{1,0:T(8,128)(2,1)S(1)} %get-tuple-element.36.terms_ref, bf16[8,1024]{1,0:T(8,128)(2,1)S(1)} %bitcast.5), custom_call_target="tpu_custom_call" | custom-call | tf_op jit(solution)/shard_map/grad_embeddings/pallas_call | solution.py:237
  75.5 3.7 %all-to-all-done.3 = bf16[64,8,128]{2,1,0:T(8,128)(2,1)S(1)} async-done(((bf16[64,8,128]{2,1,0:T(8,128)(2,1)}), bf16[64,8,128]{2,1,0:T(8,128)(2,1)S(1)}, u32[]{:S(2)}, u32[]{:S(2)}) %all-to-all-start.3) | async-done | bytes 131104 | tf_op jit(solution)/shard_map/all_to_all | solution.py:413
  79.2 0.0 collective-permute-done.3.near_ref
  79.2 4.8 %collective-permute-done.4.mid_ref = bf16[2,256,128]{2,1,0:T(8,128)(2,1)S(1)} collective-permute-done((bf16[2,256,128]{2,1,0:T(8,128)(2,1)S(1)}, bf16[2,256,128]{2,1,0:T(8,128)(2,1)S(1)}, u32[]{:S(2)}, u32[]{:S(2)}) %collective-permute-start.4) | collective-permute-done | bytes 131104 | tf_op jit(solution)/shard_map/ppermute | solution.py:397
  84.1 0.2 collective-permute-done.5.far_ref
  84.3 0.7 final.1
  (6 shorter events, 0.0 us)
Async XLA Ops:
  0.6 12.5 %copy-start.1 = (bf16[256,1024]{1,0:T(8,128)(2,1)S(1)}, bf16[256,1024]{1,0:T(8,128)(2,1)}, u32[]{:S(2)}) copy-start(bf16[256,1024]{1,0:T(8,128)(2,1)} %cot_ref.3) | copy-start | bytes 1572868
  2.7 10.4 %copy-start.3 = (bf16[2,256,128]{2,1,0:T(8,128)(2,1)S(1)}, bf16[2,256,128]{2,1,0:T(8,128)(2,1)}, u32[]{:S(2)}) copy-start(bf16[2,256,128]{2,1,0:T(8,128)(2,1)} %get-tuple-element.27.own_ref) | copy-start | bytes 393220
  2.7 10.3 %collective-permute-start.2 = (bf16[2,256,128]{2,1,0:T(8,128)(2,1)}, bf16[2,256,128]{2,1,0:T(8,128)(2,1)S(1)}, u32[]{:S(2)}, u32[]{:S(2)}) collective-permute-start(bf16[2,256,128]{2,1,0:T(8,128)(2,1)} %get-tuple-element.27.own_ref), channel_id=1, source_target_pairs={{0,24},{32,56},{64,88},{96,120},{128,152},{160,184},{192,216},{224... | collective-permute-start | bytes 393224 | tf_op jit(solution)/shard_map/ppermute | solution.py:335
  6.3 6.7 %collective-permute-start.1 = (bf16[2,256,128]{2,1,0:T(8,128)(2,1)}, bf16[2,256,128]{2,1,0:T(8,128)(2,1)S(1)}, u32[]{:S(2)}, u32[]{:S(2)}) collective-permute-start(bf16[2,256,128]{2,1,0:T(8,128)(2,1)} %get-tuple-element.27.own_ref), channel_id=1, source_target_pairs={{0,16},{8,24},{32,48},{40,56},{64,80},{72,88},{96,112},{104,120},{... | collective-permute-start | bytes 393224 | tf_op jit(solution)/shard_map/ppermute | solution.py:335
  7.6 5.4 %collective-permute-start = (bf16[2,256,128]{2,1,0:T(8,128)(2,1)}, bf16[2,256,128]{2,1,0:T(8,128)(2,1)S(1)}, u32[]{:S(2)}, u32[]{:S(2)}) collective-permute-start(bf16[2,256,128]{2,1,0:T(8,128)(2,1)} %get-tuple-element.27.own_ref), channel_id=1, source_target_pairs={{0,8},{8,16},{16,24},{32,40},{40,48},{48,56},{64,72},{72,80},{80,8... | collective-permute-start | bytes 393224 | tf_op jit(solution)/shard_map/ppermute | solution.py:335
  9.7 12.5 %all-to-all-start = ((f32[8,8,256]{2,1,0:T(8,128)}), f32[8,8,256]{2,1,0:T(8,128)S(1)}, u32[]{:S(2)}, u32[]{:S(2)}) async-start(f32[8,8,256]{2,1,0:T(8,128)} %get-tuple-element.26), calls=%async_computation | async-start | bytes 131072 | tf_op jit(solution)/shard_map/all_to_all | solution.py:336
  13.0 9.2 %copy-start.2 = (bf16[256,1024]{1,0:T(8,128)(2,1)S(1)}, bf16[256,1024]{1,0:T(8,128)(2,1)}, u32[]{:S(2)}) copy-start(bf16[256,1024]{1,0:T(8,128)(2,1)} %base_ref.1) | copy-start | bytes 1572868
  13.1 9.1 %copy-start.5 = (bf16[8,1024]{1,0:T(8,128)(2,1)S(1)}, bf16[8,1024]{1,0:T(8,128)(2,1)}, u32[]{:S(2)}) copy-start(bf16[8,1024]{1,0:T(8,128)(2,1)} %up_ref.1) | copy-start | bytes 49156
  22.2 23.2 %copy-start = (bf16[256,1024]{1,0:T(8,128)(2,1)S(1)}, bf16[256,1024]{1,0:T(8,128)(2,1)}, u32[]{:S(2)}) copy-start(bf16[256,1024]{1,0:T(8,128)(2,1)} %emb_ref.1) | copy-start | bytes 1572868
  54.9 19.3 %copy-start.4 = (bf16[1024,8]{0,1:T(8,128)(2,1)S(1)}, bf16[1024,8]{0,1:T(8,128)(2,1)}, u32[]{:S(2)}) copy-start(bf16[1024,8]{0,1:T(8,128)(2,1)} %param.8) | copy-start | bytes 49156
  54.9 24.3 %all-to-all-start.3 = ((bf16[64,8,128]{2,1,0:T(8,128)(2,1)}), bf16[64,8,128]{2,1,0:T(8,128)(2,1)S(1)}, u32[]{:S(2)}, u32[]{:S(2)}) async-start(bf16[64,8,128]{2,1,0:T(8,128)(2,1)} %spread.1), calls=%async_computation.3 | async-start | bytes 262144 | tf_op jit(solution)/shard_map/all_to_all | solution.py:413
  70.3 8.9 %collective-permute-start.3 = (bf16[2,256,128]{2,1,0:T(8,128)(2,1)S(1)}, bf16[2,256,128]{2,1,0:T(8,128)(2,1)S(1)}, u32[]{:S(2)}, u32[]{:S(2)}) collective-permute-start(bf16[2,256,128]{2,1,0:T(8,128)(2,1)S(1)} %get-tuple-element.39), channel_id=1, source_target_pairs={{8,0},{16,8},{24,16},{40,32},{48,40},{56,48},{72,64},{80,72},{88,8... | collective-permute-start | bytes 393224 | tf_op jit(solution)/shard_map/ppermute | solution.py:397
  71.6 12.5 %collective-permute-start.4 = (bf16[2,256,128]{2,1,0:T(8,128)(2,1)S(1)}, bf16[2,256,128]{2,1,0:T(8,128)(2,1)S(1)}, u32[]{:S(2)}, u32[]{:S(2)}) collective-permute-start(bf16[2,256,128]{2,1,0:T(8,128)(2,1)S(1)} %get-tuple-element.40), channel_id=1, source_target_pairs={{16,0},{24,8},{48,32},{56,40},{80,64},{88,72},{112,96},{120,104},{... | collective-permute-start | bytes 393224 | tf_op jit(solution)/shard_map/ppermute | solution.py:397
  72.9 11.3 %collective-permute-start.5 = (bf16[2,256,128]{2,1,0:T(8,128)(2,1)S(1)}, bf16[2,256,128]{2,1,0:T(8,128)(2,1)S(1)}, u32[]{:S(2)}, u32[]{:S(2)}) collective-permute-start(bf16[2,256,128]{2,1,0:T(8,128)(2,1)S(1)} %get-tuple-element.41), channel_id=1, source_target_pairs={{24,0},{56,32},{88,64},{120,96},{152,128},{184,160},{216,192},{248... | collective-permute-start | bytes 393224 | tf_op jit(solution)/shard_map/ppermute | solution.py:397

commit v4 on v2

--- a/solution.py
+++ b/solution.py
@@ -9,16 +9,12 @@
 from jax.sharding import PartitionSpec as P
 
 HD = 128
-TIE = 0
-HPS = 4
-RM = 2
-RH = 5
-FIRST_LOW = 12
-FIRST_HIGH = 0
+HEADS_PER_STEP = 8
+FIRST_HEAD = 5
+FIRST_BLOCK = 2
+FIRST_LOW, FIRST_HIGH = 12, 0
 TURN = 8
-WIDE_BACK = False
-SENT = jnp.float32
-FIRST_VMEM = 16 * 2**20
+FIRST_VMEM = 60 * 2**20
 SPAN = 4
 FAR = 1e30
 F32 = jnp.float32
@@ -46,26 +42,37 @@
     return jnp.concatenate([x, x, x, jnp.zeros_like(x)], axis=0).astype(BF16)
 
 
-def first_kernel(emb_hbm, down_hbm, parts_ref, emb_ref, down_ref, sems):
-    copies = [
-        pltpu.make_async_copy(down_hbm, down_ref, sems.at[0]),
-        pltpu.make_async_copy(emb_hbm, emb_ref, sems.at[1]),
-    ]
+def first_kernel(
+    emb_hbm, down_hbm, key_hbm, value_hbm, parts_ref, kv_ref, emb_ref, down_ref, sems
+):
+    pairs = (
+        (down_hbm, down_ref),
+        (emb_hbm, emb_ref),
+        (key_hbm, kv_ref.at[0]),
+        (value_hbm, kv_ref.at[1]),
+    )
+    copies = [pltpu.make_async_copy(a, b, sems.at[i]) for i, (a, b) in enumerate(pairs)]
     for copy in copies:
         copy.start()
-    for copy in copies:
-        copy.wait()
+    copies[0].wait()
+    copies[1].wait()
     part = dot(down_ref[...], emb_ref[...], NT)
     for peer in range(parts_ref.shape[0]):
         parts_ref[peer] = part
-
-
-def second_kernel(parts_ref, key_ref, value_ref, cot_ref, kv_ref, cot_t_ref):
-    kv_ref[0] = key_ref[...]
-    kv_ref[1] = value_ref[...]
+    copies[2].wait()
+    copies[3].wait()
+
+
+def turn_kernel(cot_ref, cot_t_ref):
     for head in range(cot_ref.shape[1] // HD):
         at = slice(head * HD, (head + 1) * HD)
         cot_t_ref[at, :] = cot_ref[:, at].astype(F32).T.astype(BF16)
+
+
+def spread_kernel(terms_ref, out_ref):
+    total = jnp.sum(terms_ref[...], axis=0)
+    for peer in range(out_ref.shape[0]):
+        out_ref[peer] = total
 
 
 def main_kernel(
@@ -226,7 +233,7 @@
     n_head, r, _ = parts.shape
     keys = SPAN * rows
     return call(
-        functools.partial(main_kernel, HPS),
+        functools.partial(main_kernel, HEADS_PER_STEP),
         [
             ((rows, width), BF16),
             ((n_head, r, rows), F32),
@@ -260,8 +267,15 @@
     )
 
 
+def spread(terms, peers):
+    (out,) = call(
+        spread_kernel, [((peers, *terms.shape[1:]), F32)], terms, name="spread"
+    )
+    return out
+
+
 def heads_of(n_ctx, n_head):
-    order = [(h + RH) % n_head for h in range(n_head)]
+    order = [(h + FIRST_HEAD) % n_head for h in range(n_head)]
     return [[c * n_head + h for h in order] for c in range(n_ctx)]
 
 
@@ -283,35 +297,34 @@
                     pairs.append(pair[::-1] if back else pair)
         return pairs
 
-    (parts,) = call(
+    parts, kv = call(
         first_kernel,
-        [((n_head, r, rows), F32)],
+        [((n_head, r, rows), F32), ((2, rows, HD), BF16)],
         embeddings,
         down_t,
-        own=(0, 1),
+        key_states,
+        values,
+        own=(0, 1, 2, 3),
         scratch=[
             pltpu.VMEM(embeddings.shape, BF16),
             pltpu.VMEM(down_t.shape, BF16),
-            pltpu.SemaphoreType.DMA((2,)),
+            pltpu.SemaphoreType.DMA((4,)),
         ],
         limit=FIRST_VMEM,
         name="inner_parts",
     )
-    kv, cot_t = call(
-        second_kernel,
-        [((2, rows, HD), BF16), ((width, rows), BF16)],
-        parts,
-        key_states,
-        values,
-        grad_out,
-        own=(0,),
-        name="pack",
+    (cot_t,) = call(
+        turn_kernel, [((width, rows), BF16)], grad_out, name="turn"
     )
     near, mid, far = (lax.ppermute(kv, both, route(d)) for d in (1, 2, 3))
     parts = lax.all_to_all(parts, both, 0, 0, axis_index_groups=heads_of(n_ctx, n_head))
     attn_out, inner_parts, part_up, grad_own, grad_near, grad_mid, grad_far = attention(
         parts, adapter_up, query_base, grad_out, cot_t, kv, near, mid, far
     )
+    sent = [
+        lax.ppermute(term, both, route(d, back=True))
+        for d, term in ((1, grad_near), (2, grad_mid), (3, grad_far))
+    ]
     inner_parts = lax.all_to_all(inner_parts, both, 0, 0, axis_index_groups=heads_of(n_ctx, n_head))
 
     wide = 16
@@ -320,15 +333,14 @@
     lists = [
         [g * wide + (m + first_of[g]) % wide for m in range(wide)] for g in range(blocks)
     ]
-    block_order = [(g + RM) % blocks for g in range(blocks)]
-    every = [[c for g in block_order for c in lists[g]]]
+    block_order = [(g + FIRST_BLOCK) % blocks for g in range(blocks)]
     apart = [[lists[g][m] for g in block_order] for m in range(wide)]
     back = [
         [g * wide + (m + first_of[g] + TURN) % wide for m in range(wide)]
         for g in range(blocks)
     ]
-    close, apart, every, back = (
-        ctx_groups(n_ctx, n_head, groups) for groups in (lists, apart, every, back)
+    close, apart, back = (
+        ctx_groups(n_ctx, n_head, groups) for groups in (lists, apart, back)
     )
     piece = 2 * width // wide
     pieces, terms = call(
@@ -347,35 +359,11 @@
         name="grad_embeddings",
     )
 
-    def send_terms(after):
-        terms = (grad_near, grad_mid, grad_far)
-        if after is not None:
-            after, *terms = lax.optimization_barrier((after, *terms))
-        sent = [
-            lax.ppermute(term, both, route(d, back=True))
-            for d, term in zip((1, 2, 3), terms)
-        ]
-        return after, sent
-
-    if TIE == 0:
-        _, sent = send_terms(None)
-    if TIE == 3:
-        _, sent = send_terms(None)
-        pieces, *sent = lax.optimization_barrier((pieces, *sent))
     pieces = lax.all_to_all(pieces, both, 0, 0, axis_index_groups=close)
-    mine = jnp.sum(pieces, axis=0)
-    if TIE == 1:
-        mine, sent = send_terms(mine)
-    if WIDE_BACK:
-        mine = jnp.broadcast_to(mine[None].astype(SENT), (n_ctx, *mine.shape))
-        whole = lax.all_to_all(mine, both, 0, 0, axis_index_groups=every)
-        whole = jnp.sum(whole.reshape(blocks, wide, r, piece).astype(F32), axis=0)
-    else:
-        mine = jnp.broadcast_to(mine[None], (blocks, *mine.shape))
-        mine = lax.all_to_all(mine, both, 0, 0, axis_index_groups=apart)
-        mine = jnp.sum(mine, axis=0)
-        mine = jnp.broadcast_to(mine[None], (wide, *mine.shape))
-        whole = lax.all_to_all(mine, both, 0, 0, axis_index_groups=back)
+    mine = spread(pieces, blocks)
+    mine = lax.all_to_all(mine, both, 0, 0, axis_index_groups=apart)
+    mine = spread(mine, wide)
+    whole = lax.all_to_all(mine, both, 0, 0, axis_index_groups=back)
     whole = whole.transpose(1, 0, 2).reshape(r, 2 * width)
     grad_adapter_down, grad_adapter_up = whole[:, :width].T, whole[:, width:]
 

time: 89.8 us -> 88.5 us (0.986)
  blocking collectives: 24.7 us -> 10.3 us
  waiting for transfers between devices: 7.05 us -> 14.9 us
  starting transfers between devices: 36.4 us -> 43.3 us
  local copies, waits for them, and re-layouts: 5.91 us -> 1.38 us
  Pallas kernels: 14.2 us -> 17.2 us
    all_to_all x1 -> x0, blocking collectives: 14.2 us -> none  [on_device(): lax.all_to_all(parts, both, 0, 0, axis_index_groups=heads_of(n_ctx, n_head))]
    all_to_all x0 -> x1, waiting for transfers between devices: none -> 7.67 us  [on_device(): lax.all_to_all(parts, both, 0, 0, axis_index_groups=heads_of(n_ctx, n_head))]
    all_to_all x0 -> x1, starting transfers between devices: none -> 6.5 us  [on_device(): lax.all_to_all(parts, both, 0, 0, axis_index_groups=heads_of(n_ctx, n_head))]
    unnamed x18 -> x12, local copies, waits for them, and re-layouts: 3.33 us -> 0.03 us
    pallas_call x5 -> x7, Pallas kernels: 14.2 us -> 17.2 us  [call(): pl.pallas_call(kernel, out_shape=[jax.ShapeDtypeStruct(shape, dtype) for...]
    broadcast_in_dim x2 -> x0, local copies, waits for them, and re-layouts: 1.23 us -> none  [the longest x1 0.62 us: on_device(): mine = jnp.broadcast_to(mine[None], (wide, *mine.shape))]
  transfers between devices with their start and end apart: 9 -> 10, of which waited for: 3 -> 4; matrix products, arithmetic and copies ran while one was open for 2% -> 1% of each run, Pallas kernels for 1% -> 3%
where the time goes in v4:
time: 88.5 us; the launch traced here: 87.9 us
  starting transfers between devices  43.3 us (49%)
  Pallas kernels  17.2 us (19%)
  waiting for transfers between devices  14.9 us (17%)
  blocking collectives  10.3 us (12%)
  local copies, waits for them, and re-layouts  1.38 us (2%)
    pallas_call x7, Pallas kernels, call(): pl.pallas_call(kernel, out_shape=[jax.ShapeDtypeStruct(shape, dtype) for...  17.2 us
    all_to_all x1, starting transfers between devices, on_device(): mine = lax.all_to_all(mine, both, 0, 0, axis_index_groups=apart)  11.2 us
    all_to_all x1, blocking collectives, on_device(): lax.all_to_all(inner_parts, both, 0, 0, axis_index_groups=heads_of(n_ctx,...  10.3 us
    ppermute x3, starting transfers between devices, on_device(): lax.ppermute(term, both, route(d, back=True))  10.1 us
    all_to_all x1, waiting for transfers between devices, on_device(): lax.all_to_all(parts, both, 0, 0, axis_index_groups=heads_of(n_ctx, n_head))  7.67 us
    all_to_all x1, starting transfers between devices, on_device(): pieces = lax.all_to_all(pieces, both, 0, 0, axis_index_groups=close)  7.37 us
    all_to_all x1, starting transfers between devices, on_device(): lax.all_to_all(parts, both, 0, 0, axis_index_groups=heads_of(n_ctx, n_head))  6.5 us
    all_to_all x1, waiting for transfers between devices, on_device(): whole = lax.all_to_all(mine, both, 0, 0, axis_index_groups=back)  4.72 us
  transfers between devices with their start and end apart: 10, of which 4 were waited for; matrix products, arithmetic and copies ran while one was open for 1% of the time, Pallas kernels for 3%

profile of v4, /device:TPU:20, one launch (start us, length us, event | category | flops | bytes accessed | tf_op | source)
XLA Modules:
  0.0 87.9 jit_solution(10491939420521846107)
XLA Ops:
  0.6 2.1 %inner_parts.1 = (f32[8,8,256]{2,1,0:T(8,128)}, bf16[2,256,128]{2,1,0:T(8,128)(2,1)}) custom-call(bf16[256,1024]{1,0:T(8,128)(2,1)} %emb_ref.1, bf16[8,1024]{1,0:T(8,128)(2,1)} %bitcast.10, bf16[256,128]{1,0:T(8,128)(2,1)} %key_hbm.1, bf16[256,128]{1,0:T(8,128)(2,1)} %value_hbm.1), custom_call_target="tpu_custom_call" | custom-call | tf_op jit(solution)/shard_map/inner_parts/pallas_call | solution.py:217
  2.7 0.7 collective-permute-start.2
  3.4 1.3 %collective-permute-start.1 = (bf16[2,256,128]{2,1,0:T(8,128)(2,1)}, bf16[2,256,128]{2,1,0:T(8,128)(2,1)S(1)}, u32[]{:S(2)}, u32[]{:S(2)}) collective-permute-start(bf16[2,256,128]{2,1,0:T(8,128)(2,1)} %get-tuple-element.18.own_ref), channel_id=1, source_target_pairs={{0,16},{8,24},{32,48},{40,56},{64,80},{72,88},{96,112},{104,120},{... | collective-permute-start | bytes 393224 | tf_op jit(solution)/shard_map/ppermute | solution.py:319
  4.7 2.4 %collective-permute-start = (bf16[2,256,128]{2,1,0:T(8,128)(2,1)}, bf16[2,256,128]{2,1,0:T(8,128)(2,1)S(1)}, u32[]{:S(2)}, u32[]{:S(2)}) collective-permute-start(bf16[2,256,128]{2,1,0:T(8,128)(2,1)} %get-tuple-element.18.own_ref), channel_id=1, source_target_pairs={{0,8},{8,16},{16,24},{32,40},{40,48},{48,56},{64,72},{72,80},{80,8... | collective-permute-start | bytes 393224 | tf_op jit(solution)/shard_map/ppermute | solution.py:319
  7.1 6.5 %all-to-all-start = ((f32[8,8,256]{2,1,0:T(8,128)}), f32[8,8,256]{2,1,0:T(8,128)S(1)}, u32[]{:S(2)}, u32[]{:S(2)}) async-start(f32[8,8,256]{2,1,0:T(8,128)} %get-tuple-element.17), calls=%async_computation | async-start | bytes 131072 | tf_op jit(solution)/shard_map/all_to_all | solution.py:320
  13.6 0.0 copy-start.2
  13.6 0.0 copy-start.3
  13.6 0.0 copy-start.5
  13.6 0.2 turn.1.cot_t_ref
  13.8 0.0 copy-start
  13.9 7.7 %all-to-all-done.parts_ref = f32[8,8,256]{2,1,0:T(8,128)S(1)} async-done(((f32[8,8,256]{2,1,0:T(8,128)}), f32[8,8,256]{2,1,0:T(8,128)S(1)}, u32[]{:S(2)}, u32[]{:S(2)}) %all-to-all-start) | async-done | bytes 65568 | tf_op jit(solution)/shard_map/all_to_all | solution.py:320
  21.5 0.0 collective-permute-done.2.far_ref
  21.5 0.5 collective-permute-done.1.mid_ref
  22.1 11.5 %attention.1 = (bf16[256,1024]{1,0:T(8,128)(2,1)}, f32[8,8,256]{2,1,0:T(8,128)S(1)}, f32[8,1024]{1,0:T(8,128)S(1)}, f32[2,256,128]{2,1,0:T(8,128)S(1)}, bf16[2,2...) custom-call(f32[8,8,256]{2,1,0:T(8,128)S(1)} %all-to-all-done.parts_ref, ...), custom_call_target="tpu_custom_call" | custom-call | tf_op jit(solution)/shard_map/attention/pallas_call | solution.py:217
  33.6 10.3 %all_to_all.25.parts_ref = f32[8,8,256]{2,1,0:T(8,128)S(1)} all-to-all(f32[8,8,256]{2,1,0:T(8,128)S(1)} %get-tuple-element.20), channel_id=1, replica_groups={{5,6,7,0,1,2,3,4},{13,14,15,8,9,10,11,12},{21,22,23,16,17,18,19,20},{29..., dimensions={0} | all-to-all | bytes 131072 | tf_op jit(solution)/shard_map/all_to_all | solution.py:328
  43.9 0.8 adapter_parts.1
  44.7 7.4 %all-to-all-start.2 = ((f32[16,8,128]{2,1,0:T(8,128)}), f32[16,8,128]{2,1,0:T(8,128)S(1)}, u32[]{:S(2)}, u32[]{:S(2)}) async-start(f32[16,8,128]{2,1,0:T(8,128)} %get-tuple-element.23), calls=%async_computation.2 | async-start | bytes 131072 | tf_op jit(solution)/shard_map/all_to_all | solution.py:362
  52.1 7.9 %collective-permute-start.3 = (bf16[2,256,128]{2,1,0:T(8,128)(2,1)S(1)}, bf16[2,256,128]{2,1,0:T(8,128)(2,1)S(1)}, u32[]{:S(2)}, u32[]{:S(2)}) collective-permute-start(bf16[2,256,128]{2,1,0:T(8,128)(2,1)S(1)} %get-tuple-element.25), channel_id=1, source_target_pairs={{8,0},{16,8},{24,16},{40,32},{48,40},{56,48},{72,64},{80,72},{88,8... | collective-permute-start | bytes 393224 | tf_op jit(solution)/shard_map/ppermute | solution.py:325
  60.0 1.5 %collective-permute-start.4 = (bf16[2,256,128]{2,1,0:T(8,128)(2,1)S(1)}, bf16[2,256,128]{2,1,0:T(8,128)(2,1)S(1)}, u32[]{:S(2)}, u32[]{:S(2)}) collective-permute-start(bf16[2,256,128]{2,1,0:T(8,128)(2,1)S(1)} %get-tuple-element.26), channel_id=1, source_target_pairs={{16,0},{24,8},{48,32},{56,40},{80,64},{88,72},{112,96},{120,104},{... | collective-permute-start | bytes 393224 | tf_op jit(solution)/shard_map/ppermute | solution.py:325
  61.5 0.7 collective-permute-start.5
  62.2 0.0 all-to-all-done.2.terms_ref
  62.2 0.6 spread.2
  62.8 11.2 %all-to-all-start.3 = ((f32[4,8,128]{2,1,0:T(8,128)}), f32[4,8,128]{2,1,0:T(8,128)S(1)}, u32[]{:S(2)}, u32[]{:S(2)}) async-start(f32[4,8,128]{2,1,0:T(8,128)} %spread.2), calls=%async_computation.3 | async-start | bytes 32768 | tf_op jit(solution)/shard_map/all_to_all | solution.py:364
  74.1 1.3 %grad_embeddings.1 = f32[256,1024]{1,0:T(8,128)} custom-call(bf16[32,256]{1,0:T(8,128)(2,1)S(1)} %get-tuple-element.22.terms_ref, bf16[8,1024]{1,0:T(8,128)(2,1)S(1)} %bitcast.11), custom_call_target="tpu_custom_call" | custom-call | tf_op jit(solution)/shard_map/grad_embeddings/pallas_call | solution.py:217
  75.4 2.0 %all-to-all-done.3.terms_ref = f32[4,8,128]{2,1,0:T(8,128)S(1)} async-done(((f32[4,8,128]{2,1,0:T(8,128)}), f32[4,8,128]{2,1,0:T(8,128)S(1)}, u32[]{:S(2)}, u32[]{:S(2)}) %all-to-all-start.3) | async-done | bytes 16416 | tf_op jit(solution)/shard_map/all_to_all | solution.py:364
  77.3 0.6 spread.3
  78.0 3.8 %all-to-all-start.4 = ((f32[16,8,128]{2,1,0:T(8,128)}), f32[16,8,128]{2,1,0:T(8,128)S(1)}, u32[]{:S(2)}, u32[]{:S(2)}) async-start(f32[16,8,128]{2,1,0:T(8,128)} %spread.3), calls=%async_computation.4 | async-start | bytes 131072 | tf_op jit(solution)/shard_map/all_to_all | solution.py:366
  81.7 0.0 collective-permute-done.3
  81.8 0.1 convert_add_fusion
  81.8 0.7 slice_bitcast_fusion
  82.5 4.7 %all-to-all-done.4 = f32[16,8,128]{2,1,0:T(8,128)S(1)} async-done(((f32[16,8,128]{2,1,0:T(8,128)}), f32[16,8,128]{2,1,0:T(8,128)S(1)}, u32[]{:S(2)}, u32[]{:S(2)}) %all-to-all-start.4) | async-done | bytes 65568 | tf_op jit(solution)/shard_map/all_to_all | solution.py:366
  87.3 0.6 fusion
  (11 shorter events, 0.0 us)
Async XLA Ops:
  0.6 13.0 %copy-start.1 = (bf16[256,1024]{1,0:T(8,128)(2,1)S(1)}, bf16[256,1024]{1,0:T(8,128)(2,1)}, u32[]{:S(2)}) copy-start(bf16[256,1024]{1,0:T(8,128)(2,1)} %cot_ref.3) | copy-start | bytes 1572868
  2.7 18.8 %collective-permute-start.2 = (bf16[2,256,128]{2,1,0:T(8,128)(2,1)}, bf16[2,256,128]{2,1,0:T(8,128)(2,1)S(1)}, u32[]{:S(2)}, u32[]{:S(2)}) collective-permute-start(bf16[2,256,128]{2,1,0:T(8,128)(2,1)} %get-tuple-element.18.own_ref), channel_id=1, source_target_pairs={{0,24},{32,56},{64,88},{96,120},{128,152},{160,184},{192,216},{224... | collective-permute-start | bytes 393224 | tf_op jit(solution)/shard_map/ppermute | solution.py:319
  3.4 18.6 %collective-permute-start.1 = (bf16[2,256,128]{2,1,0:T(8,128)(2,1)}, bf16[2,256,128]{2,1,0:T(8,128)(2,1)S(1)}, u32[]{:S(2)}, u32[]{:S(2)}) collective-permute-start(bf16[2,256,128]{2,1,0:T(8,128)(2,1)} %get-tuple-element.18.own_ref), channel_id=1, source_target_pairs={{0,16},{8,24},{32,48},{40,56},{64,80},{72,88},{96,112},{104,120},{... | collective-permute-start | bytes 393224 | tf_op jit(solution)/shard_map/ppermute | solution.py:319
  4.7 17.3 %collective-permute-start = (bf16[2,256,128]{2,1,0:T(8,128)(2,1)}, bf16[2,256,128]{2,1,0:T(8,128)(2,1)S(1)}, u32[]{:S(2)}, u32[]{:S(2)}) collective-permute-start(bf16[2,256,128]{2,1,0:T(8,128)(2,1)} %get-tuple-element.18.own_ref), channel_id=1, source_target_pairs={{0,8},{8,16},{16,24},{32,40},{40,48},{48,56},{64,72},{72,80},{80,8... | collective-permute-start | bytes 393224 | tf_op jit(solution)/shard_map/ppermute | solution.py:319
  7.1 14.4 %all-to-all-start = ((f32[8,8,256]{2,1,0:T(8,128)}), f32[8,8,256]{2,1,0:T(8,128)S(1)}, u32[]{:S(2)}, u32[]{:S(2)}) async-start(f32[8,8,256]{2,1,0:T(8,128)} %get-tuple-element.17), calls=%async_computation | async-start | bytes 131072 | tf_op jit(solution)/shard_map/all_to_all | solution.py:320
  13.6 8.4 %copy-start.2 = (bf16[256,1024]{1,0:T(8,128)(2,1)S(1)}, bf16[256,1024]{1,0:T(8,128)(2,1)}, u32[]{:S(2)}) copy-start(bf16[256,1024]{1,0:T(8,128)(2,1)} %base_ref.1) | copy-start | bytes 1572868
  13.6 8.4 %copy-start.3 = (bf16[2,256,128]{2,1,0:T(8,128)(2,1)S(1)}, bf16[2,256,128]{2,1,0:T(8,128)(2,1)}, u32[]{:S(2)}) copy-start(bf16[2,256,128]{2,1,0:T(8,128)(2,1)} %get-tuple-element.18.own_ref) | copy-start | bytes 393220
  13.6 8.4 %copy-start.5 = (bf16[8,1024]{1,0:T(8,128)(2,1)S(1)}, bf16[8,1024]{1,0:T(8,128)(2,1)}, u32[]{:S(2)}) copy-start(bf16[8,1024]{1,0:T(8,128)(2,1)} %up_ref.1) | copy-start | bytes 49156
  13.8 30.0 %copy-start = (bf16[256,1024]{1,0:T(8,128)(2,1)S(1)}, bf16[256,1024]{1,0:T(8,128)(2,1)}, u32[]{:S(2)}) copy-start(bf16[256,1024]{1,0:T(8,128)(2,1)} %emb_ref.1) | copy-start | bytes 1572868
  44.7 17.5 %all-to-all-start.2 = ((f32[16,8,128]{2,1,0:T(8,128)}), f32[16,8,128]{2,1,0:T(8,128)S(1)}, u32[]{:S(2)}, u32[]{:S(2)}) async-start(f32[16,8,128]{2,1,0:T(8,128)} %get-tuple-element.23), calls=%async_computation.2 | async-start | bytes 131072 | tf_op jit(solution)/shard_map/all_to_all | solution.py:362
  52.1 29.7 %collective-permute-start.3 = (bf16[2,256,128]{2,1,0:T(8,128)(2,1)S(1)}, bf16[2,256,128]{2,1,0:T(8,128)(2,1)S(1)}, u32[]{:S(2)}, u32[]{:S(2)}) collective-permute-start(bf16[2,256,128]{2,1,0:T(8,128)(2,1)S(1)} %get-tuple-element.25), channel_id=1, source_target_pairs={{8,0},{16,8},{24,16},{40,32},{48,40},{56,48},{72,64},{80,72},{88,8... | collective-permute-start | bytes 393224 | tf_op jit(solution)/shard_map/ppermute | solution.py:325
  60.0 21.8 %collective-permute-start.4 = (bf16[2,256,128]{2,1,0:T(8,128)(2,1)S(1)}, bf16[2,256,128]{2,1,0:T(8,128)(2,1)S(1)}, u32[]{:S(2)}, u32[]{:S(2)}) collective-permute-start(bf16[2,256,128]{2,1,0:T(8,128)(2,1)S(1)} %get-tuple-element.26), channel_id=1, source_target_pairs={{16,0},{24,8},{48,32},{56,40},{80,64},{88,72},{112,96},{120,104},{... | collective-permute-start | bytes 393224 | tf_op jit(solution)/shard_map/ppermute | solution.py:325
  61.5 20.2 %collective-permute-start.5 = (bf16[2,256,128]{2,1,0:T(8,128)(2,1)S(1)}, bf16[2,256,128]{2,1,0:T(8,128)(2,1)S(1)}, u32[]{:S(2)}, u32[]{:S(2)}) collective-permute-start(bf16[2,256,128]{2,1,0:T(8,128)(2,1)S(1)} %get-tuple-element.27), channel_id=1, source_target_pairs={{24,0},{56,32},{88,64},{120,96},{152,128},{184,160},{216,192},{248... | collective-permute-start | bytes 393224 | tf_op jit(solution)/shard_map/ppermute | solution.py:325
  62.8 11.2 %copy-start.4 = (bf16[1024,8]{0,1:T(8,128)(2,1)S(1)}, bf16[1024,8]{0,1:T(8,128)(2,1)}, u32[]{:S(2)}) copy-start(bf16[1024,8]{0,1:T(8,128)(2,1)} %param.8) | copy-start | bytes 49156
  62.8 14.5 %all-to-all-start.3 = ((f32[4,8,128]{2,1,0:T(8,128)}), f32[4,8,128]{2,1,0:T(8,128)S(1)}, u32[]{:S(2)}, u32[]{:S(2)}) async-start(f32[4,8,128]{2,1,0:T(8,128)} %spread.2), calls=%async_computation.3 | async-start | bytes 32768 | tf_op jit(solution)/shard_map/all_to_all | solution.py:364
  78.0 9.3 %all-to-all-start.4 = ((f32[16,8,128]{2,1,0:T(8,128)}), f32[16,8,128]{2,1,0:T(8,128)S(1)}, u32[]{:S(2)}, u32[]{:S(2)}) async-start(f32[16,8,128]{2,1,0:T(8,128)} %spread.3), calls=%async_computation.4 | async-start | bytes 131072 | tf_op jit(solution)/shard_map/all_to_all | solution.py:366

commit v5 on v4

--- a/solution.py
+++ b/solution.py
@@ -12,7 +12,7 @@
 HEADS_PER_STEP = 8
 FIRST_HEAD = 5
 FIRST_BLOCK = 2
-FIRST_LOW, FIRST_HIGH = 12, 0
+FIRST_LOW, FIRST_HIGH = 12, 12
 TURN = 8
 FIRST_VMEM = 60 * 2**20
 SPAN = 4

time: 88.5 us -> 87.2 us (0.985)
  waiting for transfers between devices: 14.9 us -> 13.9 us
    ppermute x3, starting transfers between devices: 10.1 us -> 9.2 us  [on_device(): lax.ppermute(term, both, route(d, back=True))]
    all_to_all x1, starting transfers between devices: 11.2 us -> 12.1 us  [on_device(): mine = lax.all_to_all(mine, both, 0, 0, axis_index_groups=apart)]
where the time goes in v5:
time: 87.2 us; the launch traced here: 86.6 us
  starting transfers between devices  42.9 us (49%)
  Pallas kernels  17.2 us (20%)
  waiting for transfers between devices  13.9 us (16%)
  blocking collectives  10.3 us (12%)
  local copies, waits for them, and re-layouts  1.38 us (2%)
    pallas_call x7, Pallas kernels, call(): pl.pallas_call(kernel, out_shape=[jax.ShapeDtypeStruct(shape, dtype) for...  17.2 us
    all_to_all x1, starting transfers between devices, on_device(): mine = lax.all_to_all(mine, both, 0, 0, axis_index_groups=apart)  12.1 us
    all_to_all x1, blocking collectives, on_device(): lax.all_to_all(inner_parts, both, 0, 0, axis_index_groups=heads_of(n_ctx,...  10.3 us
    ppermute x3, starting transfers between devices, on_device(): lax.ppermute(term, both, route(d, back=True))  9.2 us
    all_to_all x1, waiting for transfers between devices, on_device(): lax.all_to_all(parts, both, 0, 0, axis_index_groups=heads_of(n_ctx, n_head))  7.67 us
    all_to_all x1, starting transfers between devices, on_device(): pieces = lax.all_to_all(pieces, both, 0, 0, axis_index_groups=close)  7.37 us
    all_to_all x1, starting transfers between devices, on_device(): lax.all_to_all(parts, both, 0, 0, axis_index_groups=heads_of(n_ctx, n_head))  6.5 us
    all_to_all x1, waiting for transfers between devices, on_device(): whole = lax.all_to_all(mine, both, 0, 0, axis_index_groups=back)  4.64 us
  transfers between devices with their start and end apart: 10, of which 4 were waited for; matrix products, arithmetic and copies ran while one was open for 1% of the time, Pallas kernels for 3%

profile of v5, /device:TPU:20, one launch (start us, length us, event | category | flops | bytes accessed | tf_op | source)
XLA Modules:
  0.0 86.6 jit_solution(6158693576161978058)
XLA Ops:
  0.6 2.1 %inner_parts.1 = (f32[8,8,256]{2,1,0:T(8,128)}, bf16[2,256,128]{2,1,0:T(8,128)(2,1)}) custom-call(bf16[256,1024]{1,0:T(8,128)(2,1)} %emb_ref.1, bf16[8,1024]{1,0:T(8,128)(2,1)} %bitcast.10, bf16[256,128]{1,0:T(8,128)(2,1)} %key_hbm.1, bf16[256,128]{1,0:T(8,128)(2,1)} %value_hbm.1), custom_call_target="tpu_custom_call" | custom-call | tf_op jit(solution)/shard_map/inner_parts/pallas_call | solution.py:217
  2.7 0.7 collective-permute-start.2
  3.4 1.3 %collective-permute-start.1 = (bf16[2,256,128]{2,1,0:T(8,128)(2,1)}, bf16[2,256,128]{2,1,0:T(8,128)(2,1)S(1)}, u32[]{:S(2)}, u32[]{:S(2)}) collective-permute-start(bf16[2,256,128]{2,1,0:T(8,128)(2,1)} %get-tuple-element.18.own_ref), channel_id=1, source_target_pairs={{0,16},{8,24},{32,48},{40,56},{64,80},{72,88},{96,112},{104,120},{... | collective-permute-start | bytes 393224 | tf_op jit(solution)/shard_map/ppermute | solution.py:319
  4.7 2.4 %collective-permute-start = (bf16[2,256,128]{2,1,0:T(8,128)(2,1)}, bf16[2,256,128]{2,1,0:T(8,128)(2,1)S(1)}, u32[]{:S(2)}, u32[]{:S(2)}) collective-permute-start(bf16[2,256,128]{2,1,0:T(8,128)(2,1)} %get-tuple-element.18.own_ref), channel_id=1, source_target_pairs={{0,8},{8,16},{16,24},{32,40},{40,48},{48,56},{64,72},{72,80},{80,8... | collective-permute-start | bytes 393224 | tf_op jit(solution)/shard_map/ppermute | solution.py:319
  7.1 6.5 %all-to-all-start = ((f32[8,8,256]{2,1,0:T(8,128)}), f32[8,8,256]{2,1,0:T(8,128)S(1)}, u32[]{:S(2)}, u32[]{:S(2)}) async-start(f32[8,8,256]{2,1,0:T(8,128)} %get-tuple-element.17), calls=%async_computation | async-start | bytes 131072 | tf_op jit(solution)/shard_map/all_to_all | solution.py:320
  13.6 0.0 copy-start.2
  13.6 0.0 copy-start.3
  13.6 0.0 copy-start.5
  13.6 0.2 turn.1.cot_t_ref
  13.8 0.0 copy-start
  13.9 7.7 %all-to-all-done.parts_ref = f32[8,8,256]{2,1,0:T(8,128)S(1)} async-done(((f32[8,8,256]{2,1,0:T(8,128)}), f32[8,8,256]{2,1,0:T(8,128)S(1)}, u32[]{:S(2)}, u32[]{:S(2)}) %all-to-all-start) | async-done | bytes 65568 | tf_op jit(solution)/shard_map/all_to_all | solution.py:320
  21.5 0.0 collective-permute-done.2.far_ref
  21.5 0.5 collective-permute-done.1.mid_ref
  22.0 0.0 collective-permute-done.near_ref
  22.1 11.5 %attention.1 = (bf16[256,1024]{1,0:T(8,128)(2,1)}, f32[8,8,256]{2,1,0:T(8,128)S(1)}, f32[8,1024]{1,0:T(8,128)S(1)}, f32[2,256,128]{2,1,0:T(8,128)S(1)}, bf16[2,2...) custom-call(f32[8,8,256]{2,1,0:T(8,128)S(1)} %all-to-all-done.parts_ref, ...), custom_call_target="tpu_custom_call" | custom-call | tf_op jit(solution)/shard_map/attention/pallas_call | solution.py:217
  33.6 10.3 %all_to_all.25.parts_ref = f32[8,8,256]{2,1,0:T(8,128)S(1)} all-to-all(f32[8,8,256]{2,1,0:T(8,128)S(1)} %get-tuple-element.20), channel_id=1, replica_groups={{5,6,7,0,1,2,3,4},{13,14,15,8,9,10,11,12},{21,22,23,16,17,18,19,20},{29..., dimensions={0} | all-to-all | bytes 131072 | tf_op jit(solution)/shard_map/all_to_all | solution.py:328
  43.9 0.8 adapter_parts.1
  44.7 7.4 %all-to-all-start.2 = ((f32[16,8,128]{2,1,0:T(8,128)}), f32[16,8,128]{2,1,0:T(8,128)S(1)}, u32[]{:S(2)}, u32[]{:S(2)}) async-start(f32[16,8,128]{2,1,0:T(8,128)} %get-tuple-element.23), calls=%async_computation.2 | async-start | bytes 131072 | tf_op jit(solution)/shard_map/all_to_all | solution.py:362
  52.1 7.0 %collective-permute-start.3 = (bf16[2,256,128]{2,1,0:T(8,128)(2,1)S(1)}, bf16[2,256,128]{2,1,0:T(8,128)(2,1)S(1)}, u32[]{:S(2)}, u32[]{:S(2)}) collective-permute-start(bf16[2,256,128]{2,1,0:T(8,128)(2,1)S(1)} %get-tuple-element.25), channel_id=1, source_target_pairs={{8,0},{16,8},{24,16},{40,32},{48,40},{56,48},{72,64},{80,72},{88,8... | collective-permute-start | bytes 393224 | tf_op jit(solution)/shard_map/ppermute | solution.py:325
  59.1 1.5 %collective-permute-start.4 = (bf16[2,256,128]{2,1,0:T(8,128)(2,1)S(1)}, bf16[2,256,128]{2,1,0:T(8,128)(2,1)S(1)}, u32[]{:S(2)}, u32[]{:S(2)}) collective-permute-start(bf16[2,256,128]{2,1,0:T(8,128)(2,1)S(1)} %get-tuple-element.26), channel_id=1, source_target_pairs={{16,0},{24,8},{48,32},{56,40},{80,64},{88,72},{112,96},{120,104},{... | collective-permute-start | bytes 393224 | tf_op jit(solution)/shard_map/ppermute | solution.py:325
  60.6 0.7 collective-permute-start.5
  61.3 0.0 all-to-all-done.2.terms_ref
  61.3 0.6 spread.2
  61.9 12.1 %all-to-all-start.3 = ((f32[4,8,128]{2,1,0:T(8,128)}), f32[4,8,128]{2,1,0:T(8,128)S(1)}, u32[]{:S(2)}, u32[]{:S(2)}) async-start(f32[4,8,128]{2,1,0:T(8,128)} %spread.2), calls=%async_computation.3 | async-start | bytes 32768 | tf_op jit(solution)/shard_map/all_to_all | solution.py:364
  74.1 1.3 %grad_embeddings.1 = f32[256,1024]{1,0:T(8,128)} custom-call(bf16[32,256]{1,0:T(8,128)(2,1)S(1)} %get-tuple-element.22.terms_ref, bf16[8,1024]{1,0:T(8,128)(2,1)S(1)} %bitcast.11), custom_call_target="tpu_custom_call" | custom-call | tf_op jit(solution)/shard_map/grad_embeddings/pallas_call | solution.py:217
  75.4 1.1 %all-to-all-done.3.terms_ref = f32[4,8,128]{2,1,0:T(8,128)S(1)} async-done(((f32[4,8,128]{2,1,0:T(8,128)}), f32[4,8,128]{2,1,0:T(8,128)S(1)}, u32[]{:S(2)}, u32[]{:S(2)}) %all-to-all-start.3) | async-done | bytes 16416 | tf_op jit(solution)/shard_map/all_to_all | solution.py:364
  76.5 0.6 spread.3
  77.1 3.4 %all-to-all-start.4 = ((f32[16,8,128]{2,1,0:T(8,128)}), f32[16,8,128]{2,1,0:T(8,128)S(1)}, u32[]{:S(2)}, u32[]{:S(2)}) async-start(f32[16,8,128]{2,1,0:T(8,128)} %spread.3), calls=%async_computation.4 | async-start | bytes 131072 | tf_op jit(solution)/shard_map/all_to_all | solution.py:366
  80.5 0.1 convert_add_fusion
  80.6 0.7 slice_bitcast_fusion
  81.3 4.6 %all-to-all-done.4 = f32[16,8,128]{2,1,0:T(8,128)S(1)} async-done(((f32[16,8,128]{2,1,0:T(8,128)}), f32[16,8,128]{2,1,0:T(8,128)S(1)}, u32[]{:S(2)}, u32[]{:S(2)}) %all-to-all-start.4) | async-done | bytes 65568 | tf_op jit(solution)/shard_map/all_to_all | solution.py:366
  85.9 0.6 fusion
  (11 shorter events, 0.0 us)
Async XLA Ops:
  0.6 13.0 %copy-start.1 = (bf16[256,1024]{1,0:T(8,128)(2,1)S(1)}, bf16[256,1024]{1,0:T(8,128)(2,1)}, u32[]{:S(2)}) copy-start(bf16[256,1024]{1,0:T(8,128)(2,1)} %cot_ref.3) | copy-start | bytes 1572868
  2.7 18.8 %collective-permute-start.2 = (bf16[2,256,128]{2,1,0:T(8,128)(2,1)}, bf16[2,256,128]{2,1,0:T(8,128)(2,1)S(1)}, u32[]{:S(2)}, u32[]{:S(2)}) collective-permute-start(bf16[2,256,128]{2,1,0:T(8,128)(2,1)} %get-tuple-element.18.own_ref), channel_id=1, source_target_pairs={{0,24},{32,56},{64,88},{96,120},{128,152},{160,184},{192,216},{224... | collective-permute-start | bytes 393224 | tf_op jit(solution)/shard_map/ppermute | solution.py:319
  3.4 18.6 %collective-permute-start.1 = (bf16[2,256,128]{2,1,0:T(8,128)(2,1)}, bf16[2,256,128]{2,1,0:T(8,128)(2,1)S(1)}, u32[]{:S(2)}, u32[]{:S(2)}) collective-permute-start(bf16[2,256,128]{2,1,0:T(8,128)(2,1)} %get-tuple-element.18.own_ref), channel_id=1, source_target_pairs={{0,16},{8,24},{32,48},{40,56},{64,80},{72,88},{96,112},{104,120},{... | collective-permute-start | bytes 393224 | tf_op jit(solution)/shard_map/ppermute | solution.py:319
  4.7 17.3 %collective-permute-start = (bf16[2,256,128]{2,1,0:T(8,128)(2,1)}, bf16[2,256,128]{2,1,0:T(8,128)(2,1)S(1)}, u32[]{:S(2)}, u32[]{:S(2)}) collective-permute-start(bf16[2,256,128]{2,1,0:T(8,128)(2,1)} %get-tuple-element.18.own_ref), channel_id=1, source_target_pairs={{0,8},{8,16},{16,24},{32,40},{40,48},{48,56},{64,72},{72,80},{80,8... | collective-permute-start | bytes 393224 | tf_op jit(solution)/shard_map/ppermute | solution.py:319
  7.1 14.4 %all-to-all-start = ((f32[8,8,256]{2,1,0:T(8,128)}), f32[8,8,256]{2,1,0:T(8,128)S(1)}, u32[]{:S(2)}, u32[]{:S(2)}) async-start(f32[8,8,256]{2,1,0:T(8,128)} %get-tuple-element.17), calls=%async_computation | async-start | bytes 131072 | tf_op jit(solution)/shard_map/all_to_all | solution.py:320
  13.6 8.4 %copy-start.2 = (bf16[256,1024]{1,0:T(8,128)(2,1)S(1)}, bf16[256,1024]{1,0:T(8,128)(2,1)}, u32[]{:S(2)}) copy-start(bf16[256,1024]{1,0:T(8,128)(2,1)} %base_ref.1) | copy-start | bytes 1572868
  13.6 8.4 %copy-start.3 = (bf16[2,256,128]{2,1,0:T(8,128)(2,1)S(1)}, bf16[2,256,128]{2,1,0:T(8,128)(2,1)}, u32[]{:S(2)}) copy-start(bf16[2,256,128]{2,1,0:T(8,128)(2,1)} %get-tuple-element.18.own_ref) | copy-start | bytes 393220
  13.6 8.4 %copy-start.5 = (bf16[8,1024]{1,0:T(8,128)(2,1)S(1)}, bf16[8,1024]{1,0:T(8,128)(2,1)}, u32[]{:S(2)}) copy-start(bf16[8,1024]{1,0:T(8,128)(2,1)} %up_ref.1) | copy-start | bytes 49156
  13.8 30.0 %copy-start = (bf16[256,1024]{1,0:T(8,128)(2,1)S(1)}, bf16[256,1024]{1,0:T(8,128)(2,1)}, u32[]{:S(2)}) copy-start(bf16[256,1024]{1,0:T(8,128)(2,1)} %emb_ref.1) | copy-start | bytes 1572868
  44.7 16.6 %all-to-all-start.2 = ((f32[16,8,128]{2,1,0:T(8,128)}), f32[16,8,128]{2,1,0:T(8,128)S(1)}, u32[]{:S(2)}, u32[]{:S(2)}) async-start(f32[16,8,128]{2,1,0:T(8,128)} %get-tuple-element.23), calls=%async_computation.2 | async-start | bytes 131072 | tf_op jit(solution)/shard_map/all_to_all | solution.py:362
  52.1 28.4 %collective-permute-start.3 = (bf16[2,256,128]{2,1,0:T(8,128)(2,1)S(1)}, bf16[2,256,128]{2,1,0:T(8,128)(2,1)S(1)}, u32[]{:S(2)}, u32[]{:S(2)}) collective-permute-start(bf16[2,256,128]{2,1,0:T(8,128)(2,1)S(1)} %get-tuple-element.25), channel_id=1, source_target_pairs={{8,0},{16,8},{24,16},{40,32},{48,40},{56,48},{72,64},{80,72},{88,8... | collective-permute-start | bytes 393224 | tf_op jit(solution)/shard_map/ppermute | solution.py:325
  59.1 21.4 %collective-permute-start.4 = (bf16[2,256,128]{2,1,0:T(8,128)(2,1)S(1)}, bf16[2,256,128]{2,1,0:T(8,128)(2,1)S(1)}, u32[]{:S(2)}, u32[]{:S(2)}) collective-permute-start(bf16[2,256,128]{2,1,0:T(8,128)(2,1)S(1)} %get-tuple-element.26), channel_id=1, source_target_pairs={{16,0},{24,8},{48,32},{56,40},{80,64},{88,72},{112,96},{120,104},{... | collective-permute-start | bytes 393224 | tf_op jit(solution)/shard_map/ppermute | solution.py:325
  60.6 19.9 %collective-permute-start.5 = (bf16[2,256,128]{2,1,0:T(8,128)(2,1)S(1)}, bf16[2,256,128]{2,1,0:T(8,128)(2,1)S(1)}, u32[]{:S(2)}, u32[]{:S(2)}) collective-permute-start(bf16[2,256,128]{2,1,0:T(8,128)(2,1)S(1)} %get-tuple-element.27), channel_id=1, source_target_pairs={{24,0},{56,32},{88,64},{120,96},{152,128},{184,160},{216,192},{248... | collective-permute-start | bytes 393224 | tf_op jit(solution)/shard_map/ppermute | solution.py:325
  61.9 12.1 %copy-start.4 = (bf16[1024,8]{0,1:T(8,128)(2,1)S(1)}, bf16[1024,8]{0,1:T(8,128)(2,1)}, u32[]{:S(2)}) copy-start(bf16[1024,8]{0,1:T(8,128)(2,1)} %param.8) | copy-start | bytes 49156
  61.9 14.5 %all-to-all-start.3 = ((f32[4,8,128]{2,1,0:T(8,128)}), f32[4,8,128]{2,1,0:T(8,128)S(1)}, u32[]{:S(2)}, u32[]{:S(2)}) async-start(f32[4,8,128]{2,1,0:T(8,128)} %spread.2), calls=%async_computation.3 | async-start | bytes 32768 | tf_op jit(solution)/shard_map/all_to_all | solution.py:364
  77.1 8.8 %all-to-all-start.4 = ((f32[16,8,128]{2,1,0:T(8,128)}), f32[16,8,128]{2,1,0:T(8,128)S(1)}, u32[]{:S(2)}, u32[]{:S(2)}) async-start(f32[16,8,128]{2,1,0:T(8,128)} %spread.3), calls=%async_computation.4 | async-start | bytes 131072 | tf_op jit(solution)/shard_map/all_to_all | solution.py:366
